TPU v7x, 32 devices: a whole 2x2x4 slice. The times are simulated.
32 devices in a mesh: fsdp: 16 (over z, x, core), tp: 2 (over y).
Axes of the slice: x: 2, y: 2, z: 4, core: 2. Of those that a mesh axis runs over, the one named last changes fastest.
Arguments:
- tokens: bfloat16 [8192, 2048], P(('fsdp', 'tp')), may hold values from -6 to 6
- cotangent: bfloat16 [8192, 2048], P(('fsdp', 'tp')), may hold values from -6 to 6
- valid_len: int32 [16], replicated, may hold values from 256 to 512, as said below
- pic_start: int32 [16], replicated, may hold values from 0 to 256, as said below
- norm_gains: float32 [2, 2048], replicated, may hold values from 0.5 to 1.5
- norm_moment: float32 [2, 2048], replicated, may hold values from -96 to 96
- norm_square: float32 [2, 2048], replicated, may hold values from 18.0224 to 73.728
- head_gains: float32 [2, 128], replicated, may hold values from 0.5 to 1.5
- head_moment: float32 [2, 128], replicated, may hold values from -448 to 448
- head_square: float32 [2, 128], replicated, may hold values from 409.6 to 1638.4
- query_weight: float32 [2048, 2048], P('fsdp', 'tp'), may hold values from -0.125 to 0.125
- query_moment: float32 [2048, 2048], P('fsdp', 'tp'), may hold values from -112 to 112
- query_square: float32 [2048, 2048], P('fsdp', 'tp'), may hold values from 24.576 to 106.496
- keyvalue_matrix: float32 [2, 2048, 1024], P(None, 'fsdp', 'tp'), may hold values from -0.125 to 0.125
- keyvalue_first_moment: float32 [2, 2048, 1024], P(None, 'fsdp', 'tp'), may hold values from -96 to 96
- keyvalue_second_moment: float32 [2, 2048, 1024], P(None, 'fsdp', 'tp'), may hold values from 20.48 to 81.92
- headgate_weight: float32 [2048, 16], P('fsdp', 'tp'), may hold values from -0.125 to 0.125
- headgate_moment: float32 [2048, 16], P('fsdp', 'tp'), may hold values from -256 to 256
- headgate_square: float32 [2048, 16], P('fsdp', 'tp'), may hold values from 163.84 to 696.32
- output_weight: float32 [2048, 2048], P('tp', 'fsdp'), may hold values from -1.5 to 1.5
- output_moment: float32 [2048, 2048], P('tp', 'fsdp'), may hold values from -6 to 6
- output_square: float32 [2048, 2048], P('tp', 'fsdp'), may hold values from 0.08192 to 0.32768
- gateup_weight: float32 [2, 2048, 6144], P(None, 'fsdp', 'tp'), may hold values from -0.125 to 0.125
- gateup_moment: float32 [2, 2048, 6144], P(None, 'fsdp', 'tp'), may hold values from -20 to 20
- gateup_square: float32 [2, 2048, 6144], P(None, 'fsdp', 'tp'), may hold values from 0.8192 to 3.2768
- down_weight: float32 [6144, 2048], P('tp', 'fsdp'), may hold values from -0.078125 to 0.078125
- down_moment: float32 [6144, 2048], P('tp', 'fsdp'), may hold values from -32 to 32
- down_square: float32 [6144, 2048], P('tp', 'fsdp'), may hold values from 2.94912 to 11.4688
Outputs:
- block_output: bfloat16 [8192, 2048], P(('fsdp', 'tp'))
- tokens_grad: float32 [8192, 2048], P(('fsdp', 'tp'))
- branch_scales: float32 [3], replicated
- updated_norms: float32 [2, 2048], replicated
- momentum_norms: float32 [2, 2048], replicated
- variance_norms: float32 [2, 2048], replicated
- updated_heads: float32 [2, 128], replicated
- momentum_heads: float32 [2, 128], replicated
- variance_heads: float32 [2, 128], replicated
- updated_query: float32 [2048, 2048], P('fsdp', 'tp')
- momentum_query: float32 [2048, 2048], P('fsdp', 'tp')
- variance_query: float32 [2048, 2048], P('fsdp', 'tp')
- updated_keyvalue: float32 [2, 2048, 1024], P(None, 'fsdp', 'tp')
- momentum_keyvalue: float32 [2, 2048, 1024], P(None, 'fsdp', 'tp')
- variance_keyvalue: float32 [2, 2048, 1024], P(None, 'fsdp', 'tp')
- updated_headgate: float32 [2048, 16], P('fsdp', 'tp')
- momentum_headgate: float32 [2048, 16], P('fsdp', 'tp')
- variance_headgate: float32 [2048, 16], P('fsdp', 'tp')
- updated_output: float32 [2048, 2048], P('tp', 'fsdp')
- momentum_output: float32 [2048, 2048], P('tp', 'fsdp')
- variance_output: float32 [2048, 2048], P('tp', 'fsdp')
- updated_gateup: float32 [2, 2048, 6144], P(None, 'fsdp', 'tp')
- momentum_gateup: float32 [2, 2048, 6144], P(None, 'fsdp', 'tp')
- variance_gateup: float32 [2, 2048, 6144], P(None, 'fsdp', 'tp')
- updated_down: float32 [6144, 2048], P('tp', 'fsdp')
- momentum_down: float32 [6144, 2048], P('tp', 'fsdp')
- variance_down: float32 [6144, 2048], P('tp', 'fsdp')
Inputs may be any that keep to these rules, and one draw needn't show every extreme that they name: The first valid_len[s] tokens of sequence s are valid, the rest are padding; some sequence has all 512 tokens valid. Sequence s holds one picture piece of 256 tokens from pic_start[s], with pic_start[s] + 256 <= valid_len[s].
All inputs are finite; a program needn't handle non-finite values.
Results may differ from a plain program's by a relative error of at most 0.012.
Values may be sent and summed in bfloat16 or wider, within the bound.
A program may use at most 384 MiB of HBM per device.

v0:
```python
import jax
import jax.numpy as jnp
from jax import lax
from jax.experimental import pallas as pl
from jax.experimental.pallas import tpu as pltpu
from jax.sharding import Mesh
from jax.sharding import PartitionSpec as P

MODEL_WIDTH = 2048
QUERY_HEADS = 16
HEAD_WIDTH = 128
FF = 6144
PIC = 256
STEP = 10

norm_epsilon = 1e-06
rope_base = 1000000.0
beta_first = 0.9
beta_second = 0.999
adam_epsilon = 1e-08
weight_decay = 0.1
masked_score = -1e30
low = jnp.bfloat16
wide = jnp.float32


def normalize(values, scaling):
    return (
        values
        * lax.rsqrt(jnp.mean(values * values, axis=-1, keepdims=True) + norm_epsilon)
        * scaling
    )


def norm_back(values, scaling, upstream):
    factor = lax.rsqrt(jnp.mean(values * values, axis=-1, keepdims=True) + norm_epsilon)
    weighted = upstream * scaling
    projected = jnp.mean(weighted * values, axis=-1, keepdims=True)
    result = factor * weighted - values * (factor * factor * factor) * projected
    return (result, jnp.sum(upstream * values * factor, axis=tuple(range(values.ndim - 1))))


def rotary_tables(length_value):
    halves = HEAD_WIDTH // 2
    frequency = rope_base ** (-(jnp.arange(halves, dtype=wide) * 2.0 / HEAD_WIDTH))
    angles = jnp.arange(length_value, dtype=wide)[:, None] * frequency[None, :]
    cosine, sine = jnp.cos(angles), jnp.sin(angles)
    return (
        jnp.concatenate([cosine, cosine], axis=1),
        jnp.concatenate([-sine, sine], axis=1),
    )


def adam_update(weight, moment, square, gradient, step_rate, decay_rate):
    moment_new = beta_first * moment + (1.0 - beta_first) * gradient
    square_new = beta_second * square + (1.0 - beta_second) * gradient * gradient
    bias_first = 1.0 - beta_first**STEP
    bias_second = 1.0 - beta_second**STEP
    update = moment_new / bias_first / (jnp.sqrt(square_new / bias_second) + adam_epsilon)
    return (weight - step_rate * (update + decay_rate * weight), moment_new, square_new)


def dot(left, right, left_dim, right_dim):
    return lax.dot_general(
        left, right, (((left_dim,), (right_dim,)), ((), ())), preferred_element_type=wide
    )


def fetch(parts):
    pieces = []
    for core in range(2):
        for part in parts:
            size = part.shape[1] // 2
            pieces.append(part[:, core * size : (core + 1) * size].astype(low))
    count = len(parts)
    local_block = jnp.stack(
        [jnp.concatenate(pieces[core * count : (core + 1) * count], axis=1) for core in range(2)]
    )
    return lax.all_gather(local_block, ("w", "c"), axis=1, tiled=True)


def columns_of(both, start, size):
    return lax.dynamic_slice(
        both, (lax.axis_index("c"), 0, start), (1, both.shape[1], size)
    ).reshape(both.shape[1], size)


MESH = pl.DeviceIdType.MESH
BLOCKS = 4
STRIP = 16
ANY = pl.BlockSpec(memory_space=pl.ANY)
VMEM = pl.BlockSpec(memory_space=pltpu.VMEM)


def ring_place(index, count):
    odd = lax.rem(index, 2)
    pair = lax.div(index, 2)
    return (1 - odd) * pair + odd * (count - 1 - pair)


def ring_index(place, count):
    late = lax.div(place, count // 2)
    return (1 - late) * 2 * place + late * (2 * (count - 1 - place) + 1)


class Device:
    def __init__(self, semaphores):
        self.w, self.c, self.t = (lax.axis_index(axis) for axis in ("w", "c", "t"))
        self.count = lax.axis_size("w")
        self.place = ring_place(self.w, self.count)
        self.semaphores = semaphores
        self.used = 0
        self.other_core = {"c": 1 - self.c}
        self.other_row = {"t": 1 - self.t}

    def owner(self, distance):
        return ring_index(lax.rem(self.place + distance + self.count, self.count), self.count)

    def meet(self, partners):
        barrier = pltpu.get_barrier_semaphore()
        for partner in partners:
            pl.semaphore_signal(barrier, inc=1, device_id=partner, device_id_type=MESH)
        pl.semaphore_wait(barrier, len(partners))

    def remote(self, source, target, device):
        slot = self.used
        self.used += 1
        return pltpu.make_async_remote_copy(
            src_ref=source,
            dst_ref=target,
            send_sem=self.semaphores.at[0, slot],
            recv_sem=self.semaphores.at[1, slot],
            device_id=device,
            device_id_type=MESH,
        )

    def inside(self, source, target):
        slot = self.used
        self.used += 1
        return pltpu.make_async_copy(source, target, self.semaphores.at[0, slot])


def rows_at(start, size):
    return pl.ds(pl.multiple_of(start, STRIP), size)


class Spread:
    def __init__(self, device, full):
        self.device, self.full = device, full
        self.size = full.shape[0] // 4
        self.block = self.size // BLOCKS
        self.rows, self.core, self.passed, self.kept = {}, {}, {}, {}

    def where(self, core, row, index):
        return self.full.at[
            rows_at((core * 2 + row) * self.size + index * self.block, self.block)
        ]

    def put(self, index, source):
        device = self.device
        target = self.where(device.c, device.t, index)
        self.rows[index] = device.remote(source, target, device.other_row)
        self.core[index] = device.remote(source, target, device.other_core)
        self.kept[index] = device.inside(source, target)
        for copy in (self.rows[index], self.core[index], self.kept[index]):
            copy.start()

    def forward(self, index):
        device = self.device
        self.rows[index].wait_recv()
        place = self.where(device.c, 1 - device.t, index)
        self.passed[index] = device.remote(place, place, device.other_core)
        self.passed[index].start()

    def finish(self):
        for index in range(BLOCKS):
            self.rows[index].wait_send()
            self.core[index].wait()
            self.passed[index].wait()
            self.kept[index].wait()


class Collect:
    def __init__(self, device, partial, near, far, sent, came):
        self.device = device
        self.partial, self.near, self.far, self.sent, self.came = partial, near, far, sent, came
        self.size = partial.shape[0] // 4
        self.block = self.size // BLOCKS
        self.core, self.rows = {}, {}

    def start(self):
        device = self.device
        self.load = device.inside(
            self.partial.at[rows_at(device.c * 2 * self.size, 2 * self.size)], self.near
        )
        for part, row in enumerate((1 - device.t, device.t)):
            for index in range(BLOCKS):
                start = row * self.size + index * self.block
                copy = device.remote(
                    self.partial.at[rows_at((1 - device.c) * 2 * self.size + start, self.block)],
                    self.far.at[rows_at(start, self.block)],
                    device.other_core,
                )
                copy.start()
                self.core[part, index] = copy
        self.load.start()

    def pass_on(self, index):
        device = self.device
        if index == 0:
            self.load.wait()
        self.core[0, index].wait_recv()

        @pl.loop(0, self.block // STRIP)
        def _(strip):
            at = index * self.block + strip * STRIP
            rows = rows_at((1 - device.t) * self.size + at, STRIP)
            total = self.near[rows, :].astype(wide) + self.far[rows, :].astype(wide)
            self.sent[rows_at(at, STRIP), :] = total.astype(low)

        place = rows_at(index * self.block, self.block)
        self.rows[index] = device.remote(
            self.sent.at[place], self.came.at[place], device.other_row
        )
        self.rows[index].start()

    def take(self, index, use):
        device = self.device
        self.core[1, index].wait_recv()
        self.rows[index].wait_recv()

        @pl.loop(0, self.block // STRIP)
        def _(strip):
            at = index * self.block + strip * STRIP
            rows = rows_at(device.t * self.size + at, STRIP)
            mine = rows_at(at, STRIP)
            total = (
                self.near[rows, :].astype(wide)
                + self.far[rows, :].astype(wide)
                + self.came[mine, :].astype(wide)
            )
            use(mine, total)

    def finish(self):
        for index in range(BLOCKS):
            self.core[0, index].wait_send()
            self.core[1, index].wait_send()
            self.rows[index].wait_send()


class Given:
    parts = 2

    def __init__(self, grads):
        self.rows, self.columns = grads.shape
        self.grads = grads

    def take(self, starts, size):
        return [self.grads[rows_at(start, size), :].astype(wide) for start in starts]

    def sources(self, starts, size, keep):
        return [self.grads.at[rows_at(start, size)] for start in starts]


class Product:
    parts = 1

    def __init__(self, left, right, start, columns):
        self.rows, self.columns = left.shape[1], columns
        self.left, self.right, self.start = left, right, start

    def take(self, starts, size):
        left = jnp.concatenate(
            [self.left[:, pl.ds(pl.multiple_of(start, 128), size)] for start in starts], axis=1
        )
        both = dot(left, self.right[:, self.start : self.start + self.columns], 0, 0)
        return [both[:size], both[size:]]

    def sources(self, starts, size, keep):
        for way, value in enumerate(self.take(starts, size)):
            keep[way] = value.astype(low)
        return [keep.at[way] for way in range(2)]


class RingSum:
    def __init__(self, device, grads, ready, scratch, sums):
        self.device, self.grads, self.sums = device, grads, sums
        self.ready = ready
        self.slots, self.totals, self.first = scratch
        self.half = grads.rows // device.count // 2
        self.parts = grads.parts
        self.part = self.half // self.parts
        self.copies = {}
        self.ticks = [
            (step, part) for step in range(device.count) for part in range(self.parts)
        ]

    def own(self, way, distance, part):
        owner = self.device.owner(-(1 - 2 * way) * distance)
        return (owner * 2 + way) * self.half + part * self.part

    def slot(self, way, step, part):
        return self.slots.at[
            way * (self.device.count - 1) + step, pl.ds(part * self.part, self.part)
        ]

    def send(self, way, step, part, source):
        device = self.device
        copy = device.remote(
            source, self.slot(way, step, part), {"w": device.owner(1 - 2 * way)}
        )
        copy.start()
        self.copies[way, step, part] = copy

    def tick(self, count=1):
        device = self.device
        for _ in range(count):
            if not self.ticks:
                return
            step, part = self.ticks.pop(0)
            starts = [self.own(way, step + 1, part) for way in range(2)]
            if step == 0:
                self.ready()
                sources = self.grads.sources(starts, self.part, self.first)
                for way in range(2):
                    self.send(way, step, part, sources[way])
                continue
            own = self.grads.take(starts, self.part)
            for way in range(2):
                self.copies[way, step - 1, part].wait_recv()
                slot = self.slot(way, step - 1, part)
                total = (slot[...].astype(wide) + own[way]).astype(low)
                if step < device.count - 1:
                    slot[...] = total
                    self.send(way, step, part, slot)
                else:
                    self.totals[way, pl.ds(part * self.part, self.part), :] = total

    def close(self):
        device = self.device
        self.tick(len(self.ticks))
        self.away = device.remote(
            self.totals.at[1 - device.c], self.sums.at[device.c], device.other_core
        )
        self.kept = device.inside(self.totals.at[device.c], self.sums.at[device.c])
        self.away.start()
        self.kept.start()

    def finish(self):
        for copy in self.copies.values():
            copy.wait_send()
        self.away.wait()
        self.kept.wait()


def ring_shapes(columns, count):
    half = MODEL_WIDTH // count // 2
    return [
        pltpu.VMEM((2 * (count - 1), half, columns), low),
        pltpu.VMEM((2, half, columns), low),
        pltpu.VMEM((2, half, columns), low),
    ]


class RingWork:
    def __init__(self, pairs):
        self.columns = [columns for _, _, _, columns in pairs]
        self.fit = (MODEL_WIDTH // lax.axis_size("w") // 2) % 128 == 0
        self.operands, self.places = [], []
        for left, right, start, columns in pairs:
            if self.fit:
                self.places.append((self.add(left), self.add(right), start, columns))
            else:
                part = right[:, start : start + columns]
                self.places.append((self.add(dot(left, part, 0, 0).astype(low)),))

    def add(self, value):
        for index, other in enumerate(self.operands):
            if other is value:
                return index
        self.operands.append(value)
        return len(self.operands) - 1

    def begin(self, device, operands, scratch, sums):
        count = len(self.operands)
        buffers, scratch = scratch[:count], scratch[count:]
        loads = [device.inside(value, buffer) for value, buffer in zip(operands, buffers)]
        for load in loads:
            load.start()
        waiting = set(range(count))
        rings = []
        for index, place in enumerate(self.places):
            used = place[:2] if self.fit else place[:1]

            def ready(used=used):
                for number in used:
                    if number in waiting:
                        waiting.remove(number)
                        loads[number].wait()

            refs = [buffers[number] for number in used]
            grads = Product(*refs, *place[2:]) if self.fit else Given(*refs)
            rings.append(
                RingSum(device, grads, ready, scratch[3 * index : 3 * index + 3], sums[index])
            )
        return Rings(rings)

    def outputs(self):
        half = MODEL_WIDTH // lax.axis_size("w") // 2
        return [jax.ShapeDtypeStruct((2, half, size), low) for size in self.columns]

    def scratch(self):
        count = lax.axis_size("w")
        return [pltpu.VMEM(value.shape, value.dtype) for value in self.operands] + [
            shape for size in self.columns for shape in ring_shapes(size, count)
        ]

    def semaphores(self):
        return 4 * (lax.axis_size("w") + 1) * len(self.columns) + len(self.operands)


def collect_shapes(size):
    return [
        pltpu.VMEM((2 * size, MODEL_WIDTH), low),
        pltpu.VMEM((2 * size, MODEL_WIDTH), low),
        pltpu.VMEM((size, MODEL_WIDTH), low),
        pltpu.VMEM((size, MODEL_WIDTH), low),
    ]


def semaphores_for(count):
    return pltpu.SemaphoreType.DMA((2, count))


def settings(collective):
    return pltpu.CompilerParams(
        collective_id=collective, has_side_effects=True, vmem_limit_bytes=56 * 2**20
    )


def neighbours(device):
    return [
        device.other_core,
        device.other_row,
        {"w": device.owner(1)},
        {"w": device.owner(-1)},
    ]


class RingGather:
    def __init__(self, device, mine, other, full, target):
        self.device, self.full, self.target = device, full, target
        self.size = mine.shape[0]
        self.parts = min(4, self.size // STRIP)
        self.part = self.size // self.parts
        self.here = (device.w * 2 + device.c) * self.size
        here = rows_at(self.here, self.size)
        self.kept = device.inside(mine, full.at[here])
        self.crossed = device.remote(other, full.at[here], device.other_core)
        self.copies = {}
        self.stores = []
        self.ticks = [
            (step, part) for step in range(device.count - 1) for part in range(self.parts)
        ]

    def start(self):
        self.kept.start()
        self.crossed.start()

    def store(self, start, size):
        place = rows_at(start, size)
        copy = self.device.inside(self.full.at[place], self.target.at[place])
        copy.start()
        self.stores.append(copy)

    def ready(self):
        self.kept.wait()
        self.crossed.wait()
        self.store(self.device.w * 2 * self.size, 2 * self.size)

    def begin(self, way, step, part):
        owner = self.device.owner(-(1 - 2 * way) * step)
        return (owner * 2 + way) * self.size + part * self.part

    def tick(self, count=1):
        device = self.device
        for _ in range(count):
            if not self.ticks:
                return
            step, part = self.ticks.pop(0)
            for way in range(2):
                start = self.begin(way, step, part)
                block = self.full.at[rows_at(start, self.part)]
                if step > 0:
                    self.copies[way, step - 1, part].wait_recv()
                copy = device.remote(block, block, {"w": device.owner(1 - 2 * way)})
                copy.start()
                self.copies[way, step, part] = copy
                if step > 0:
                    self.store(start, self.part)

    def finish(self):
        self.tick(len(self.ticks))
        last = self.device.count - 1
        for part in range(self.parts):
            for way in range(2):
                self.copies[way, last - 1, part].wait_recv()
                self.store(self.begin(way, last, part), self.part)
        for copy in self.copies.values():
            copy.wait_send()
        for copy in self.stores:
            copy.wait()


def gather_kernel(pieces, first, second, target, first_full, second_full, full, semaphores):
    device = Device(semaphores)
    device.meet(neighbours(device))
    gather = RingGather(device, pieces.at[0], pieces.at[1], full, target)
    gather.start()
    spreads = []
    for rows, target in ((first, first_full), (second, second_full)):
        spread = Spread(device, target)
        block = spread.block
        for index in range(BLOCKS):
            spread.put(index, rows.at[pl.ds(index * block, block)])
        spreads.append(spread)
    gather.ready()
    for spread in spreads:
        for index in range(BLOCKS):
            gather.tick(gather.parts)
            spread.forward(index)
    gather.finish()
    for spread in spreads:
        spread.finish()


def gather_attention(pieces, first, second):
    count = lax.axis_size("w")
    rows = first.shape[0] * 4
    return pl.pallas_call(
        gather_kernel,
        out_shape=[
            jax.ShapeDtypeStruct((MODEL_WIDTH, pieces.shape[2]), low),
            jax.ShapeDtypeStruct((rows, MODEL_WIDTH), low),
            jax.ShapeDtypeStruct((rows, MODEL_WIDTH), low),
        ],
        in_specs=[VMEM] * 3,
        out_specs=[ANY] * 3,
        scratch_shapes=[
            pltpu.VMEM((MODEL_WIDTH, pieces.shape[2]), low),
            semaphores_for(16 * count + 8 * BLOCKS + 4),
        ],
        compiler_params=settings(1),
        cost_estimate=pl.CostEstimate(flops=0, bytes_accessed=64 * 2**20, transcendentals=0),
        name="gather_attention",
    )(pieces, first, second)


def counted_rows(device, valid, at, size):
    place = device.t * size + at.start + lax.broadcasted_iota(jnp.int32, (at.size, 1), 0)
    return jnp.where(place < valid[device.w * 2 + device.c], 1.0, 0.0)


def forward_kernel(
    valid, partial, rows, gain, pieces, middle, squares, full, target,
    near, far, sent, came, normed, gathered, semaphores,
):
    device = Device(semaphores)
    device.meet(neighbours(device))
    collect = Collect(device, partial, near, far, sent, came)
    spread = Spread(device, full)
    gather = RingGather(device, pieces.at[0], pieces.at[1], gathered, target)
    collect.start()
    gather.start()
    squares[...] = jnp.zeros_like(squares)
    collect.pass_on(0)
    gather.ready()
    gather.tick(gather.parts)
    for index in range(1, BLOCKS):
        collect.pass_on(index)

    def use(at, value):
        row = rows[at, :].astype(wide)
        counted = counted_rows(device, valid, at, rows.shape[0])
        squares[0:1, :] += jnp.sum(counted * row * row, axis=0, keepdims=True)
        squares[1:2, :] += jnp.sum(counted * value * value, axis=0, keepdims=True)
        total = row + value
        middle[at, :] = total
        normed[at, :] = normalize(total, gain[...]).astype(low)

    for index in range(BLOCKS):
        collect.take(index, use)
        spread.put(index, normed.at[pl.ds(index * spread.block, spread.block)])
        gather.tick(2)
    gather.tick(4)
    for index in range(BLOCKS):
        spread.forward(index)
        gather.tick(2)
    gather.finish()
    spread.finish()
    collect.finish()


SCALARS = pl.BlockSpec(memory_space=pltpu.SMEM)


def exchange_forward(valid, partial, rows, gain, pieces):
    size = rows.shape[0]
    count = lax.axis_size("w")
    return pl.pallas_call(
        forward_kernel,
        out_shape=[
            jax.ShapeDtypeStruct((size, MODEL_WIDTH), wide),
            jax.ShapeDtypeStruct((2, MODEL_WIDTH), wide),
            jax.ShapeDtypeStruct((4 * size, MODEL_WIDTH), low),
            jax.ShapeDtypeStruct((MODEL_WIDTH, pieces.shape[2]), low),
        ],
        in_specs=[SCALARS, ANY, VMEM, VMEM, VMEM],
        out_specs=[VMEM, VMEM, ANY, ANY],
        scratch_shapes=collect_shapes(size)
        + [
            pltpu.VMEM((size, MODEL_WIDTH), low),
            pltpu.VMEM((MODEL_WIDTH, pieces.shape[2]), low),
            semaphores_for(16 * BLOCKS + 16 * count + 4),
        ],
        compiler_params=settings(2),
        cost_estimate=pl.CostEstimate(flops=0, bytes_accessed=64 * 2**20, transcendentals=0),
        name="exchange_forward",
    )(valid, partial, rows, gain, pieces)


class Rings:
    def __init__(self, rings):
        self.rings = rings
        self.next = 0

    def tick(self, count=1):
        for _ in range(count):
            ring = self.rings[self.next]
            self.next = (self.next + 1) % len(self.rings)
            ring.tick()

    def finish(self):
        while any(ring.ticks for ring in self.rings):
            self.tick()
        for ring in self.rings:
            ring.close()
        for ring in self.rings:
            ring.finish()


def norm_back_rows(values, gain, upstream):
    factor = lax.rsqrt(jnp.mean(values * values, axis=-1, keepdims=True) + norm_epsilon)
    weighted = upstream * gain
    projected = jnp.mean(weighted * values, axis=-1, keepdims=True)
    result = factor * weighted - values * (factor * factor * factor) * projected
    return result, jnp.sum(upstream * values * factor, axis=0, keepdims=True)


def backward_kernel(work, valid, partial, output, middle, rows, gain, *refs):
    count = len(work.columns)
    operands, refs = refs[: len(work.operands)], refs[len(work.operands) :]
    grad, gain_grad, block, squares, full, refs = *refs[:5], refs[5:]
    sums, refs = refs[:count], refs[count:]
    rounded = refs[8]
    device = Device(refs[-1])
    rings = work.begin(device, operands, refs[9:-1], sums)
    device.meet(neighbours(device))
    collect = Collect(device, partial, *refs[:4])
    output_collect = Collect(device, output, *refs[4:8])
    spread = Spread(device, full)
    collect.start()
    rings.tick(2)
    gain_grad[...] = jnp.zeros_like(gain_grad)
    squares[...] = jnp.zeros_like(squares)
    for index in range(BLOCKS):
        collect.pass_on(index)
    rings.tick(count - 2)
    output_collect.start()

    def use(at, upstream):
        result, gained = norm_back_rows(middle[at, :], gain[...], upstream)
        result = result + rows[at, :].astype(wide)
        grad[at, :] = result
        rounded[at, :] = result.astype(low)
        gain_grad[...] += gained

    def use_output(at, value):
        block[at, :] = (middle[at, :] + value).astype(low)
        counted = counted_rows(device, valid, at, middle.shape[0])
        squares[...] += jnp.sum(counted * value * value, axis=0, keepdims=True)

    for index in range(BLOCKS):
        collect.take(index, use)
        spread.put(index, rounded.at[pl.ds(index * spread.block, spread.block)])
        rings.tick(1)
    for index in range(BLOCKS):
        output_collect.pass_on(index)
    rings.tick(2)
    for index in range(BLOCKS):
        spread.forward(index)
        rings.tick(1)
    for index in range(BLOCKS):
        output_collect.take(index, use_output)
        rings.tick(1)
    rings.finish()
    spread.finish()
    collect.finish()
    output_collect.finish()


def exchange_backward(valid, partial, output, middle, rows, gain, pairs):
    size = rows.shape[0]
    work = RingWork(pairs)

    def body(*refs):
        backward_kernel(work, *refs)

    return pl.pallas_call(
        body,
        out_shape=[
            jax.ShapeDtypeStruct((size, MODEL_WIDTH), wide),
            jax.ShapeDtypeStruct((1, MODEL_WIDTH), wide),
            jax.ShapeDtypeStruct((size, MODEL_WIDTH), low),
            jax.ShapeDtypeStruct((1, MODEL_WIDTH), wide),
            jax.ShapeDtypeStruct((4 * size, MODEL_WIDTH), low),
            *work.outputs(),
        ],
        in_specs=[SCALARS, ANY, ANY] + [VMEM] * 3 + [ANY] * len(work.operands),
        out_specs=[VMEM] * 4 + [ANY] * (1 + len(work.columns)),
        scratch_shapes=collect_shapes(size) * 2
        + [pltpu.VMEM((size, MODEL_WIDTH), low)]
        + work.scratch()
        + [semaphores_for(32 * BLOCKS + work.semaphores())],
        compiler_params=settings(3),
        cost_estimate=pl.CostEstimate(flops=0, bytes_accessed=128 * 2**20, transcendentals=0),
        name="exchange_backward",
    )(valid, partial, output, middle, rows, gain, *work.operands)


class Total:
    def __init__(self, device, mine, crossed, gathered):
        self.device, self.mine = device, mine
        self.crossed, self.gathered = crossed, gathered
        self.copies = {}
        self.steps = [("c", 0), ("t", 0)] + [("w", step) for step in range(device.count // 2)]

    def tick(self):
        device = self.device
        if not self.steps:
            return
        axis, step = self.steps.pop(0)
        if axis != "w":
            slot = 0 if axis == "c" else 1
            partner = device.other_core if axis == "c" else device.other_row
            copy = device.remote(self.mine.at[slot], self.crossed.at[slot], partner)
            copy.start()
            copy.wait()
            total = self.mine[slot] + self.crossed[slot]
            if slot == 0:
                self.mine[1] = total
            else:
                self.gathered[device.w] = total
            return
        for way in range(2):
            if way == 1 and step == device.count // 2 - 1:
                continue
            if step > 0:
                self.copies[way, step - 1].wait_recv()
            block = self.gathered.at[device.owner(-(1 - 2 * way) * step)]
            copy = device.remote(block, block, {"w": device.owner(1 - 2 * way)})
            copy.start()
            self.copies[way, step] = copy

    def finish(self, target):
        while self.steps:
            self.tick()
        half = self.device.count // 2
        self.copies[0, half - 1].wait_recv()
        self.copies[1, half - 2].wait_recv()
        for copy in self.copies.values():
            copy.wait_send()
        target[...] = self.gathered[0]
        for index in range(1, self.device.count):
            target[...] += self.gathered[index]


def last_kernel(
    work, first, tokens, gain, middle_grad, gain_grad, head_grads, output_squares, squares, *refs
):
    count = len(work.columns)
    operands, refs = refs[: len(work.operands)], refs[len(work.operands) :]
    first_total, stats_total, refs = refs[0], refs[1], refs[2:]
    sums, scratch = refs[:count], refs[count:]
    device = Device(scratch[-1])
    rings = work.begin(device, operands, scratch[7:-1], sums)
    device.meet(neighbours(device))
    collect = Collect(device, first, *scratch[:4])
    mine, crossed, gathered = scratch[4:7]
    total = Total(device, mine, crossed, gathered)
    mine[0] = jnp.zeros(mine.shape[1:], wide)
    mine[0, 1:2, :] = gain_grad[...]
    for row in range(2):
        mine[0, 2:3, head_at(row)] = head_grads[row : row + 1, :]
    mine[0, 3:4, :] = output_squares[...]
    mine[0, 4:6, :] = squares[...]
    collect.start()
    rings.tick(2)
    for index in range(BLOCKS):
        collect.pass_on(index)
    rings.tick(count - 2)

    def use(at, upstream):
        result, gained = norm_back_rows(tokens[at, :].astype(wide), gain[...], upstream)
        first_total[at, :] = result + middle_grad[at, :]
        mine[0, 0:1, :] += gained

    for index in range(BLOCKS):
        collect.take(index, use)
        rings.tick(1)
    while total.steps:
        total.tick()
        rings.tick(1)
    rings.finish()
    total.finish(stats_total)
    collect.finish()


def exchange_last(first, tokens, gain, middle_grad, sums, pairs):
    size = tokens.shape[0]
    count = lax.axis_size("w")
    stats = (8, MODEL_WIDTH)
    work = RingWork(pairs)

    def body(*refs):
        last_kernel(work, *refs)

    return pl.pallas_call(
        body,
        out_shape=[
            jax.ShapeDtypeStruct((size, MODEL_WIDTH), wide),
            jax.ShapeDtypeStruct(stats, wide),
            *work.outputs(),
        ],
        in_specs=[ANY] + [VMEM] * (3 + len(sums)) + [ANY] * len(work.operands),
        out_specs=[VMEM] * 2 + [ANY] * len(work.columns),
        scratch_shapes=collect_shapes(size)
        + [
            pltpu.VMEM((2, *stats), wide),
            pltpu.VMEM((2, *stats), wide),
            pltpu.VMEM((count, *stats), wide),
        ]
        + work.scratch()
        + [semaphores_for(16 * BLOCKS + 2 * count + 4 + work.semaphores())],
        compiler_params=settings(4),
        cost_estimate=pl.CostEstimate(flops=0, bytes_accessed=128 * 2**20, transcendentals=0),
        name="exchange_last",
    )(first, tokens, gain, middle_grad, *sums, *work.operands)


FEEDFORWARD_ROWS = 256
FEEDFORWARD_COLUMNS = 512


def feedforward_kernel(
    sizes, core, rows, upstream, large, small, gate_out, up_out, hidden_out, back_out, down_out
):
    weights = [(large.at[0], 0, sizes[0]), (small, sizes[0], sizes[1])]
    for weight, base, size in weights:
        for start in range(0, size, FEEDFORWARD_COLUMNS):
            width = min(FEEDFORWARD_COLUMNS, size - start)
            columns = slice(base + start, base + start + width)
            gate_part = dot(rows[...], weight[:, start : start + width], 1, 0)
            up_part = dot(rows[...], weight[:, size + start : size + start + width], 1, 0)
            hidden_grad = dot(
                upstream[...], weight[:, 2 * size + start : 2 * size + start + width], 1, 0
            )
            sigmoid_gate = jax.nn.sigmoid(gate_part)
            silu_gate = gate_part * sigmoid_gate
            hidden_out[:, columns] = (silu_gate * up_part).astype(low)
            gate_out[:, columns] = (
                hidden_grad * up_part * sigmoid_gate * (1.0 + gate_part * (1.0 - sigmoid_gate))
            ).astype(low)
            up_out[:, columns] = (hidden_grad * silu_gate).astype(low)
    for start in range(0, MODEL_WIDTH, FEEDFORWARD_COLUMNS):
        across = slice(start, start + FEEDFORWARD_COLUMNS)
        back = 0.0
        down = 0.0
        for weight, base, size in weights:
            columns = slice(base, base + size)
            back = back + dot(gate_out[:, columns], weight[across, :size], 1, 1)
            back = back + dot(up_out[:, columns], weight[across, size : 2 * size], 1, 1)
            down = down + dot(hidden_out[:, columns], weight[across, 2 * size :], 1, 1)
        back_out[:, across] = back.astype(low)
        down_out[:, across] = down.astype(low)


def feedforward(core, rows, upstream, large, small):
    sizes = (large.shape[2] // 3, small.shape[1] // 3)
    count = rows.shape[0]
    hidden = sum(sizes)

    def body(*refs):
        feedforward_kernel(sizes, *refs)

    def block(columns):
        return pl.BlockSpec((FEEDFORWARD_ROWS, columns), lambda index, core: (index, 0))

    once = pl.Buffered(1)
    return pl.pallas_call(
        body,
        grid_spec=pltpu.PrefetchScalarGridSpec(
            num_scalar_prefetch=1,
            grid=(count // FEEDFORWARD_ROWS,),
            in_specs=[
                block(MODEL_WIDTH),
                block(MODEL_WIDTH),
                pl.BlockSpec(
                    (1, *large.shape[1:]),
                    lambda index, core: (core[0], 0, 0),
                    pipeline_mode=once,
                ),
                pl.BlockSpec(small.shape, lambda index, core: (0, 0), pipeline_mode=once),
            ],
            out_specs=[block(hidden)] * 3 + [block(MODEL_WIDTH)] * 2,
        ),
        out_shape=[jax.ShapeDtypeStruct((count, hidden), low)] * 3
        + [jax.ShapeDtypeStruct((count, MODEL_WIDTH), low)] * 2,
        compiler_params=pltpu.CompilerParams(vmem_limit_bytes=52 * 2**20),
        cost_estimate=pl.CostEstimate(
            flops=12 * count * MODEL_WIDTH * hidden,
            bytes_accessed=48 * 2**20,
            transcendentals=count * hidden,
        ),
        name="feedforward",
    )(core, rows, upstream, large, small)


def head_rows(values, gain, cosine, sine):
    factor = lax.rsqrt(jnp.mean(values * values, axis=-1, keepdims=True) + norm_epsilon)
    normed = values * factor * gain
    return (normed * cosine + pltpu.roll(normed, HEAD_WIDTH // 2, 1) * sine).astype(low)


def head_back(values, gain, cosine, sine, upstream):
    turned = upstream * cosine - pltpu.roll(upstream, HEAD_WIDTH // 2, 1) * sine
    return norm_back_rows(values, gain, turned)


def head_at(index):
    return slice(index * HEAD_WIDTH, (index + 1) * HEAD_WIDTH)


def gate_column(logits, head):
    lanes = lax.broadcasted_iota(jnp.int32, logits.shape, 1)
    logit = jnp.sum(jnp.where(lanes == head, logits, 0.0), axis=-1, keepdims=True)
    return jax.nn.sigmoid(logit)


def probabilities(queries, keys, start, valid_count, piece_start):
    raw = dot(queries, keys, 1, 1) * HEAD_WIDTH ** (-0.5)
    row = start + lax.broadcasted_iota(jnp.int32, raw.shape, 0)
    column = lax.broadcasted_iota(jnp.int32, raw.shape, 1)
    last = piece_start + PIC
    inside = (row >= piece_start) & (row < last) & (column >= piece_start) & (column < last)
    allowed = (column < valid_count) & ((column <= row) | inside)
    scores = jnp.where(allowed, raw, masked_score)
    expos = jnp.exp(scores - jnp.max(scores, axis=-1, keepdims=True))
    return expos * (1.0 / jnp.sum(expos, axis=-1, keepdims=True))


QUERY_ROWS = 256


def attention_forward_kernel(
    groups, share, valid, start, rows_in, weights, gains, cosine, sine, pre, gated, partial
):
    sequence = pl.program_id(0)
    heads = groups * share
    length, projected = pre.shape
    for column in range(0, projected, 3 * HEAD_WIDTH):
        columns = slice(column, min(column + 3 * HEAD_WIDTH, projected))
        pre[:, columns] = dot(rows_in[...], weights[:, columns], 1, 0)
    for group in range(groups):
        keys = head_rows(pre[:, head_at(heads + group)], gains[1:2, :], cosine[...], sine[...])
        values = pre[:, head_at(heads + groups + group)].astype(low)
        for head in range(group * share, (group + 1) * share):
            for at in range(0, length, QUERY_ROWS):
                rows = slice(at, at + QUERY_ROWS)
                queries = head_rows(
                    pre[rows, head_at(head)], gains[0:1, :], cosine[rows, :], sine[rows, :]
                )
                probs = probabilities(queries, keys, at, valid[sequence], start[sequence])
                mixed = dot(probs.astype(low), values, 1, 0)
                gate = gate_column(pre[rows, head_at(heads + 2 * groups)], head)
                gated[rows, head_at(head)] = (mixed * gate).astype(low)
    for column in range(0, MODEL_WIDTH, 512):
        partial[:, column : column + 512] = dot(
            gated[...], weights[column : column + 512, projected:], 1, 1
        ).astype(low)


def attention_backward_kernel(
    groups, share, valid, start, pre, rows_in, weights, gains, cosine, sine,
    grads, gain_grads, partial, upstream,
):
    sequence = pl.program_id(0)
    heads = groups * share
    length, projected = pre.shape
    upstream[...] = dot(rows_in[...], weights[:, projected:], 1, 0)
    scale = HEAD_WIDTH ** (-0.5)

    @pl.when(sequence == 0)
    def _():
        gain_grads[...] = jnp.zeros_like(gain_grads)

    logit_grads = [jnp.zeros((QUERY_ROWS, HEAD_WIDTH), wide)] * (length // QUERY_ROWS)
    for group in range(groups):
        key_pre = pre[:, head_at(heads + group)]
        keys = head_rows(key_pre, gains[1:2, :], cosine[...], sine[...])
        values = pre[:, head_at(heads + groups + group)].astype(low)
        value_grad = jnp.zeros((length, HEAD_WIDTH), wide)
        key_grad = jnp.zeros((length, HEAD_WIDTH), wide)
        for head in range(group * share, (group + 1) * share):
            for block, at in enumerate(range(0, length, QUERY_ROWS)):
                rows = slice(at, at + QUERY_ROWS)
                query_pre = pre[rows, head_at(head)]
                queries = head_rows(query_pre, gains[0:1, :], cosine[rows, :], sine[rows, :])
                probs = probabilities(queries, keys, at, valid[sequence], start[sequence])
                probs_low = probs.astype(low)
                mixed = dot(probs_low, values, 1, 0)
                gate = gate_column(pre[rows, head_at(heads + 2 * groups)], head)
                gated_grad = upstream[rows, head_at(head)]
                mixed_grad = (gated_grad * gate).astype(low)
                logit_grad = (
                    jnp.sum(gated_grad * mixed, axis=-1, keepdims=True) * gate * (1.0 - gate)
                )
                lanes = lax.broadcasted_iota(jnp.int32, (QUERY_ROWS, HEAD_WIDTH), 1)
                logit_grads[block] = logit_grads[block] + jnp.where(lanes == head, logit_grad, 0.0)
                value_grad = value_grad + dot(probs_low, mixed_grad, 0, 0)
                prob_grad = dot(mixed_grad, values, 1, 1)
                score_grad = (
                    probs * (prob_grad - jnp.sum(prob_grad * probs, axis=-1, keepdims=True))
                ).astype(low)
                key_grad = key_grad + dot(score_grad, queries, 0, 0)
                query_grad, gained = head_back(
                    query_pre,
                    gains[0:1, :],
                    cosine[rows, :],
                    sine[rows, :],
                    dot(score_grad, keys, 1, 0) * scale,
                )
                grads[rows, head_at(head)] = query_grad.astype(low)
                gain_grads[0:1, :] += gained
        key_grad, gained = head_back(
            key_pre, gains[1:2, :], cosine[...], sine[...], key_grad * scale
        )
        gain_grads[1:2, :] += gained
        grads[:, head_at(heads + group)] = key_grad.astype(low)
        grads[:, head_at(heads + groups + group)] = value_grad.astype(low)
    for block, at in enumerate(range(0, length, QUERY_ROWS)):
        grads[slice(at, at + QUERY_ROWS), head_at(heads + 2 * groups)] = logit_grads[block].astype(
            low
        )
    for column in range(0, MODEL_WIDTH, 512):
        partial[:, column : column + 512] = dot(
            grads[...], weights[column : column + 512, :projected], 1, 1
        ).astype(low)


def sequence_block(columns, length):
    return pl.BlockSpec((length, columns), lambda sequence: (sequence, 0))


def fixed_block(*shape):
    return pl.BlockSpec(shape, lambda sequence: (0, 0))


def attention_call(body, name, specs, sequences, outputs, out_specs, scratch, operands):
    return pl.pallas_call(
        body,
        grid=(sequences,),
        out_shape=outputs,
        in_specs=[SCALARS, SCALARS, *specs],
        out_specs=out_specs,
        scratch_shapes=scratch,
        compiler_params=pltpu.CompilerParams(vmem_limit_bytes=52 * 2**20),
        cost_estimate=pl.CostEstimate(
            flops=2**33, bytes_accessed=24 * 2**20, transcendentals=2**21
        ),
        name=name,
    )(*operands)


def attention_specs(weights, length):
    return [
        pl.BlockSpec(weights.shape, lambda sequence: (0, 0), pipeline_mode=pl.Buffered(1)),
        fixed_block(2, HEAD_WIDTH),
        fixed_block(length, HEAD_WIDTH),
        fixed_block(length, HEAD_WIDTH),
    ]


def attention_forward(groups, share, valid, start, rows, weights, gains, cosine, sine):
    length, columns = cosine.shape[0], groups * share * HEAD_WIDTH
    projected, count = weights.shape[1] - columns, rows.shape[0]

    def body(*refs):
        attention_forward_kernel(groups, share, *refs)

    return attention_call(
        body,
        "attention_forward",
        [sequence_block(MODEL_WIDTH, length), *attention_specs(weights, length)],
        count // length,
        [
            jax.ShapeDtypeStruct((count, projected), wide),
            jax.ShapeDtypeStruct((count, columns), low),
            jax.ShapeDtypeStruct((count, MODEL_WIDTH), low),
        ],
        [sequence_block(size, length) for size in (projected, columns, MODEL_WIDTH)],
        [],
        (valid, start, rows, weights, gains, cosine, sine),
    )


def attention_backward(groups, share, valid, start, pre, rows, weights, gains, cosine, sine):
    length, columns = cosine.shape[0], groups * share * HEAD_WIDTH
    count, projected = pre.shape

    def body(*refs):
        attention_backward_kernel(groups, share, *refs)

    return attention_call(
        body,
        "attention_backward",
        [
            sequence_block(projected, length),
            sequence_block(MODEL_WIDTH, length),
            *attention_specs(weights, length),
        ],
        count // length,
        [
            jax.ShapeDtypeStruct((count, projected), low),
            jax.ShapeDtypeStruct((2, HEAD_WIDTH), wide),
            jax.ShapeDtypeStruct((count, MODEL_WIDTH), low),
        ],
        [
            sequence_block(projected, length),
            fixed_block(2, HEAD_WIDTH),
            sequence_block(MODEL_WIDTH, length),
        ],
        [pltpu.VMEM((length, columns), wide)],
        (valid, start, pre, rows, weights, gains, cosine, sine),
    )


def adam_kernel(layouts, names, heads, *refs):
    given, refs = refs[: len(names)], refs[len(names) :]
    count = len(layouts)
    stats, inverse, refs = refs[0], refs[1], refs[2:]
    extra, states, refs = refs[:11], refs[11 : 11 + 3 * count], refs[11 + 3 * count :]
    scales, refs = refs[0], refs[1:]
    extra_targets, targets, refs = refs[:11], refs[11 : 11 + 3 * count], refs[11 + 3 * count :]
    buffers, extra_buffers, refs = refs[: 3 * count], refs[3 * count :][:11], refs[3 * count + 11 :]
    small = extra_buffers[2:]
    sources, semaphores, sum_semaphores = dict(zip(names, refs)), refs[-2], refs[-1]
    fetches = [
        pltpu.make_async_copy(value, sources[name], sum_semaphores.at[0, i])
        for i, (name, value) in enumerate(zip(names, given))
    ]
    for i in range(11):
        slot = len(names) + i
        fetches.append(
            pltpu.make_async_copy(extra[i], extra_buffers[i], sum_semaphores.at[0, slot])
        )
    moves = [
        pltpu.make_async_copy(extra_buffers[i], extra_targets[i], sum_semaphores.at[1, i])
        for i in range(11)
    ]
    loads = [
        pltpu.make_async_copy(states[i], buffers[i], semaphores.at[0, i]) for i in range(3 * count)
    ]
    stores = [
        pltpu.make_async_copy(buffers[i], targets[i], semaphores.at[1, i])
        for i in range(3 * count)
    ]
    for copy in (*fetches, *loads):
        copy.start()
    for copy in fetches:
        copy.wait()
    for copy in moves[:2]:
        copy.start()

    def update(part, at, gradient, rate, decay_rate):
        old = [small[3 * part + i][at] for i in range(3)]
        for i, value in enumerate(adam_update(*old, gradient, rate, decay_rate)):
            small[3 * part + i][at] = value

    everything = (slice(None), slice(None))
    update(0, everything, stats[0:2, :], 0.5, 0.0)
    for row in range(2):
        update(1, (slice(row, row + 1), slice(None)), stats[2:3, head_at(row)], 0.5, 0.0)
    column, size = heads
    gradient = jnp.concatenate(
        [
            sources["projected"][core, :, column : column + HEAD_WIDTH].astype(wide).T[:size]
            for core in range(2)
        ],
        axis=0,
    )
    update(2, everything, gradient, layouts[0][1], weight_decay)
    for copy in moves[2:]:
        copy.start()
    lanes = lax.broadcasted_iota(jnp.int32, scales.shape, 1)
    squares = jnp.zeros(scales.shape, wide)
    for lane, row in enumerate((4, 5, 3)):
        squares = jnp.where(
            lanes == lane, jnp.sum(stats[row : row + 1, :], axis=-1, keepdims=True), squares
        )
    scales[...] = jnp.sqrt(squares * inverse[...])
    for number, (transposed, rate, leads) in enumerate(layouts):
        matrix = buffers[3 * number : 3 * number + 3]
        for load in loads[3 * number : 3 * number + 3]:
            load.wait()
        for lead, pieces in enumerate(leads):
            quarter = sum(size for _, _, size in pieces)
            for core in range(2):
                start = core * quarter
                for name, column, size in pieces:
                    step = 256 if size % 256 == 0 else 128

                    @pl.loop(0, size // step)
                    def _(block):
                        columns = pl.ds(pl.multiple_of(column + block * step, 128), step)
                        gradient = sources[name][core, :, columns].astype(wide)
                        place = pl.ds(pl.multiple_of(start + block * step, 128), step)
                        if transposed:
                            gradient = gradient.T
                            at = (place, slice(None))
                        elif len(leads) > 1:
                            at = (lead, slice(None), place)
                        else:
                            at = (slice(None), place)
                        weight, moment, square = (part[at] for part in matrix)
                        for part, value in zip(
                            matrix,
                            adam_update(weight, moment, square, gradient, rate, weight_decay),
                        ):
                            part[at] = value

                    start += size
        for store in stores[3 * number : 3 * number + 3]:
            store.start()
    for copy in (*stores, *moves):
        copy.wait()


def adam_matrices(layouts, heads, sums, stats, inverse, passed, small, states):
    def body(*refs):
        adam_kernel(layouts, list(sums), heads, *refs)

    extra = [*passed, *small]

    def like(values):
        return [jax.ShapeDtypeStruct(value.shape, value.dtype) for value in values]

    return pl.pallas_call(
        body,
        out_shape=like([inverse, *extra, *states]),
        in_specs=[ANY] * len(sums) + [VMEM] * 2 + [ANY] * (len(extra) + len(states)),
        out_specs=[VMEM] + [ANY] * (len(extra) + len(states)),
        scratch_shapes=[
            pltpu.VMEM(value.shape, value.dtype) for value in (*states, *extra, *sums.values())
        ]
        + [
            pltpu.SemaphoreType.DMA((2, len(states))),
            pltpu.SemaphoreType.DMA((2, len(sums) + len(extra))),
        ],
        compiler_params=pltpu.CompilerParams(vmem_limit_bytes=48 * 2**20),
        cost_estimate=pl.CostEstimate(
            flops=2**25, bytes_accessed=40 * 2**20, transcendentals=2**21
        ),
        name="adam_matrices",
    )(*sums.values(), stats, inverse, *extra, *states)


def prepare_kernel(
    sizes, query, keyvalue, headgate, output, gateup, down, tokens, gain,
    attention, normed, large, small,
):
    core = lax.axis_index("c")
    head_cols, group_cols = query.shape[1] // 2, keyvalue.shape[2] // 2
    edges = [head_cols, head_cols + group_cols, head_cols + 2 * group_cols]
    heads = head_cols // HEAD_WIDTH
    rows = query.shape[0]
    hidden = sum(sizes)
    logits = jnp.concatenate(
        [headgate[...], jnp.zeros((HEAD_WIDTH - headgate.shape[0], rows), wide)], axis=0
    ).T
    lanes = lax.broadcasted_iota(jnp.int32, logits.shape, 1)
    for quarter in range(2):
        slot = lax.rem(quarter + core, 2)
        columns = slice(quarter * head_cols, (quarter + 1) * head_cols)
        attention[slot, :, :head_cols] = query[:, columns].astype(low)
        for part in range(2):
            attention[slot, :, edges[part] : edges[part + 1]] = keyvalue[
                part, :, quarter * group_cols : (quarter + 1) * group_cols
            ].astype(low)
        turned = pltpu.roll(logits, HEAD_WIDTH - heads, 1) if quarter else logits
        attention[slot, :, edges[2] : edges[2] + HEAD_WIDTH] = jnp.where(
            lanes < heads, turned, 0.0
        ).astype(low)
        attention[slot, :, edges[2] + HEAD_WIDTH :] = output[columns, :].T.astype(low)
        base = quarter * hidden
        for part in range(3):
            start = 0
            for target, size in ((large.at[quarter], sizes[0]), (small.at[slot], sizes[1])):
                here = slice(base + start, base + start + size)
                value = gateup[part, :, here] if part < 2 else down[here, :].T
                target[:, part * size : (part + 1) * size] = value.astype(low)
                start += size

    @pl.loop(0, tokens.shape[0] // STRIP)
    def _(strip):
        at = rows_at(strip * STRIP, STRIP)
        normed[at, :] = normalize(tokens[at, :].astype(wide), gain[...]).astype(low)


def prepare(sizes, query, keyvalue, headgate, output, gateup, down, tokens, gain):
    rows = query.shape[0]
    columns = query.shape[1] // 2 * 2 + keyvalue.shape[2] + HEAD_WIDTH

    def body(*refs):
        prepare_kernel(sizes, *refs)

    return pl.pallas_call(
        body,
        out_shape=[
            jax.ShapeDtypeStruct((2, rows, columns), low),
            jax.ShapeDtypeStruct(tokens.shape, low),
            jax.ShapeDtypeStruct((2, rows, 3 * sizes[0]), low),
            jax.ShapeDtypeStruct((2, rows, 3 * sizes[1]), low),
        ],
        in_specs=[VMEM] * 8,
        out_specs=[VMEM] * 4,
        compiler_params=pltpu.CompilerParams(vmem_limit_bytes=48 * 2**20),
        cost_estimate=pl.CostEstimate(
            flops=2**22, bytes_accessed=12 * 2**20, transcendentals=0
        ),
        name="prepare",
    )(query, keyvalue, headgate, output, gateup, down, tokens, gain)


def local(
    tokens,
    cotangent,
    valid_len,
    pic_start,
    norm_gains,
    norm_moment,
    norm_square,
    head_gains,
    head_moment,
    head_square,
    query_weight,
    query_moment,
    query_square,
    keyvalue_matrix,
    keyvalue_first_moment,
    keyvalue_second_moment,
    headgate_weight,
    headgate_moment,
    headgate_square,
    output_weight,
    output_moment,
    output_square,
    gateup_weight,
    gateup_moment,
    gateup_square,
    down_weight,
    down_moment,
    down_square,
):
    local_rows = tokens.shape[0]
    length_value = local_rows * 2
    rows = length_value * 2
    group = lax.axis_index("w")
    core = lax.axis_index("c")
    place = lax.axis_index("t")
    heads_here = query_weight.shape[1] // HEAD_WIDTH // 2
    groups_here = keyvalue_matrix.shape[2] // HEAD_WIDTH // 2
    share = heads_here // groups_here
    head_cols = heads_here * HEAD_WIDTH
    group_cols = groups_here * HEAD_WIDTH
    hidden_here = gateup_weight.shape[2] // 2

    bounds = [0, head_cols, group_cols, group_cols, 128, head_cols]
    edges = [sum(bounds[: i + 1]) for i in range(6)]
    sizes = (hidden_here - hidden_here // 6, hidden_here // 6)
    attention_pieces, normed, large_block, small_pieces = prepare(
        sizes,
        query_weight,
        keyvalue_matrix,
        headgate_weight.T,
        output_weight,
        gateup_weight,
        down_weight,
        tokens,
        norm_gains[0:1],
    )
    large_both = lax.all_gather(large_block, ("w", "c"), axis=1, tiled=True)
    attention_full, first_full, output_grad_full = gather_attention(
        attention_pieces, normed, cotangent
    )
    valid_pair = lax.dynamic_slice_in_dim(valid_len, 2 * group, 2)
    start_pair = lax.dynamic_slice_in_dim(pic_start, 2 * group, 2)
    cosine, sine = rotary_tables(length_value)
    projected, gated_low, attention_partial = attention_forward(
        groups_here,
        share,
        valid_pair,
        start_pair,
        first_full,
        attention_full,
        head_gains,
        cosine,
        sine,
    )
    middle, squares, second_full, small_full = exchange_forward(
        valid_len, attention_partial, tokens, norm_gains[1:2], small_pieces
    )
    gate_grad, up_grad, hidden_low, second_partial, feedforward_partial = feedforward(
        core[None], second_full, output_grad_full, large_both, small_full
    )
    half = hidden_here // 2
    pieces = [(0, half), (half, hidden_here - half)]
    middle_grad, second_gain_grad, block_output, output_squares, attention_grad, *sums = (
        exchange_backward(
            valid_len,
            second_partial,
            feedforward_partial,
            middle,
            cotangent,
            norm_gains[1:2],
            [(second_full, grad, *piece) for grad in (gate_grad, up_grad) for piece in pieces],
        )
    )
    projected_grad, head_gain_grads, first_partial = attention_backward(
        groups_here,
        share,
        valid_pair,
        start_pair,
        projected,
        attention_grad,
        attention_full,
        head_gains,
        cosine,
        sine,
    )
    tokens_grad, stats, *more = exchange_last(
        first_partial,
        tokens,
        norm_gains[0:1],
        middle_grad,
        [second_gain_grad, head_gain_grads, output_squares, squares],
        [
            *((output_grad_full, hidden_low, *piece) for piece in pieces),
            (first_full, projected_grad, 0, edges[4]),
            (attention_grad, gated_low, 0, head_cols),
        ],
    )
    denominator = jnp.sum(valid_len).astype(wide) * MODEL_WIDTH
    inverse = jnp.full((1, HEAD_WIDTH), 1.0 / denominator)
    input_rate = MODEL_WIDTH ** (-0.5)
    down_rate = FF ** (-0.5)
    output_rate = max(QUERY_HEADS * HEAD_WIDTH // 128, 4) ** (-0.5)
    widths = [half, hidden_here - half]

    def parts_of(name):
        return [(f"{name} {index}", 0, width) for index, width in enumerate(widths)]

    layouts = [
        (
            False,
            input_rate,
            [parts_of("gate"), parts_of("up")],
        ),
        (True, down_rate, [parts_of("down")]),
        (False, input_rate, [[("projected", edges[0], head_cols)]]),
        (
            False,
            input_rate,
            [[("projected", edges[1], group_cols)], [("projected", edges[2], group_cols)]],
        ),
        (True, output_rate, [[("output", 0, head_cols)]]),
    ]
    names = ["gate 0", "gate 1", "up 0", "up 1", "down 0", "down 1", "projected", "output"]
    sums = dict(zip(names, [*sums, *more]))
    scales, block_output, tokens_grad, *updated = adam_matrices(
        layouts,
        (edges[3], heads_here),
        sums,
        stats,
        inverse,
        [block_output, tokens_grad],
        [
            norm_gains,
            norm_moment,
            norm_square,
            head_gains,
            head_moment,
            head_square,
            headgate_weight.T,
            headgate_moment.T,
            headgate_square.T,
        ],
        [
            gateup_weight,
            gateup_moment,
            gateup_square,
            down_weight,
            down_moment,
            down_square,
            query_weight,
            query_moment,
            query_square,
            keyvalue_matrix,
            keyvalue_first_moment,
            keyvalue_second_moment,
            output_weight,
            output_moment,
            output_square,
        ],
    )
    norms_new, heads_new, headgate_new, gateup_new, down_new, query_new, keyvalue_new, output_new = (
        updated[3 * i : 3 * i + 3] for i in range(8)
    )
    branch_scales = scales[0, :3]
    return (
        block_output,
        tokens_grad,
        branch_scales,
        *norms_new,
        *heads_new,
        *query_new,
        *keyvalue_new,
        *(value.T for value in headgate_new),
        *output_new,
        *gateup_new,
        *down_new,
    )


def solution(mesh):
    fsdp, tp = mesh.devices.shape
    fine = Mesh(mesh.devices.reshape(fsdp // 2, 2, tp), ("w", "c", "t"))
    whole = ("w", "c")
    rows = P(("w", "c", "t"), None)
    first = P(whole, "t")
    second = P(None, whole, "t")
    last = P("t", whole)
    matrices = (first,) * 3 + (second,) * 3 + (first,) * 3 + (last,) * 3 + (second,) * 3 + (last,) * 3
    return jax.shard_map(
        local,
        mesh=fine,
        in_specs=(rows, rows, P(), P()) + (P(),) * 6 + matrices,
        out_specs=(rows, rows, P()) + (P(),) * 6 + matrices,
        check_vma=False,
    )
```

profile of v0, /device:TPU:0, one launch (start us, length us, event | category | flops | bytes accessed | tf_op | source)
XLA Modules:
  0.0 670.7 jit_solution(14071990517591276342)
XLA Ops:
  7.2 0.0 all-gather.2.cloned.1.call-start
  7.2 1.4 fusion.3
  8.7 1.2 copy-done
  9.9 1.0 copy-done.1
  10.9 1.0 copy-done.3
  12.0 1.0 copy-done.5
  13.0 0.7 copy-done.26
  13.7 6.0 prepare.1
  19.7 1.0 copy-done.7
  20.7 0.9 copy-done.8
  21.6 0.7 copy-done.13
  22.4 0.6 reduce_sum.9
  23.0 0.1 dynamic_slice.6.refs_0_
  23.1 0.1 dynamic_slice.7.refs_1_
  23.8 141.1 %gather_attention.1 = (bf16[2048,1664]{1,0:T(8,128)(2,1)}, bf16[1024,2048]{1,0:T(8,128)(2,1)}, bf16[1024,2048]{1,0:T(8,128)(2,1)}) custom-call(bf16[2,128,1664]{2,1,0:T(8,128)(2,1)} %copy-done.8, bf16[256,2048]{1,0:T(8,128)(2,1)} %copy-done.7, bf16[256,2048]{1,0:T(8,128)(2,1)} %refs_4_.5), custom_call_target="tpu_custom_call" | custom-call | bytes 67108864 | tf_op jit(solution)/shard_map/gather_attention/pallas_call | solution.py:540
  165.0 1.0 fusion.2
  166.0 0.2 pad_maximum_fusion
  166.2 22.3 %attention_forward.1 = (f32[1024,1152]{1,0:T(8,128)}, bf16[1024,512]{1,0:T(8,128)(2,1)S(1)}, bf16[1024,2048]{1,0:T(8,128)(2,1)}) custom-call(s32[2]{0:T(128)S(1)} %dynamic_slice.6.refs_0_, s32[2]{0:T(128)S(1)} %dynamic_slice.7.refs_1_, bf16[1024,2048]{1,0:T(8,128)(2,1)} %get-tuple-element.93.refs_2_.refs_10_, ...), custom_call_target="tpu_custom_call" | custom-call | flops 8589934592 | bytes 25165824 | tf_op jit(solution)/shard_map/attention_forward/pallas_call | solution.py:1080
  188.5 1.0 copy-done.6
  189.5 77.0 %exchange_forward.1 = (f32[256,2048]{1,0:T(8,128)}, f32[2,2048]{1,0:T(2,128)}, bf16[1024,2048]{1,0:T(8,128)(2,1)}, bf16[2048,768]{1,0:T(8,128)(2,1)}) custom-call(s32[16]{0:T(128)} %refs_0_.3, bf16[1024,2048]{1,0:T(8,128)(2,1)} %get-tuple-element.95.partial, bf16[256,2048]{1,0:T(8,128)(2,1)} %refs_1_.3, f32[1,2048]{1,0:T(1,128)} %get-tuple-element.155.gain.refs_5_, ...), custom_call_target="tpu_custom_call" | custom-call | bytes 67108864 | tf_op jit(solution)/shard_map/exchange_forward/pallas_call | solution.py:610
  266.4 10.1 %all-gather.2.cloned.1.call-done.refs_3_ = bf16[2,2048,3840]{2,1,0:T(8,128)(2,1)} async-done(((bf16[2,128,3840]{2,1,0:T(8,128)(2,1)}), bf16[2,2048,3840]{2,1,0:T(8,128)(2,1)}) %all-gather.2.cloned.1.call-update) | async-done | bytes 31457296 | tf_op jit(solution)/shard_map/all_gather | solution.py:1412
  276.6 49.5 %feedforward.1 = (bf16[1024,1536]{1,0:T(8,128)(2,1)}, bf16[1024,1536]{1,0:T(8,128)(2,1)}, bf16[1024,1536]{1,0:T(8,128)(2,1)}, bf16[1024,2048]{1,0:T(8,128)(2,1)}, bf16[1024,2048]{1,0:T(8,128)(2,1)}) custom-call(s32[1]{0:T(128)} %bitcast.refs_0_, bf16[1024,2048]{1,0:T(8,128)(2,1)} %get-tuple-element.97.refs_1_.refs_6_, ...), custom_call_target="tpu_custom_call" | custom-call | flops 38654705664 | bytes 50331648 | tf_op jit(solution)/shard_map/feedforward/pallas_call | solution.py:910
  326.1 135.5 %exchange_backward.1 = (f32[256,2048]{1,0:T(8,128)}, f32[1,2048]{1,0:T(1,128)}, bf16[256,2048]{1,0:T(8,128)(2,1)}, f32[1,2048]{1,0:T(1,128)}, bf16[1024,2048]{1,...) custom-call(s32[16]{0:T(128)} %refs_0_.3, ...), custom_call_target="tpu_custom_call" | custom-call | bytes 134217728 | tf_op jit(solution)/shard_map/exchange_backward/pallas_call | solution.py:719
  461.6 35.1 %attention_backward.1 = (bf16[1024,1152]{1,0:T(8,128)(2,1)}, f32[2,128]{1,0:T(2,128)S(1)}, bf16[1024,2048]{1,0:T(8,128)(2,1)}) custom-call(s32[2]{0:T(128)S(1)} %dynamic_slice.6.refs_0_, s32[2]{0:T(128)S(1)} %dynamic_slice.7.refs_1_, f32[1024,1152]{1,0:T(8,128)} %get-tuple-element.110.refs_2_, bf16[1024,2048]{1,0:T(8,128)(2,1)} %get-tuple-element.111.refs_3_.refs_12_, ...), custom_call_target="tpu_custom_call" | custom-call | flops 8589934592 | bytes 25165824 | tf_op jit(solution)/shard_map/attention_backward/pallas_call | solution.py:1080
  496.7 0.6 copy-done.33
  497.4 144.7 %exchange_last.1 = (f32[256,2048]{1,0:T(8,128)}, f32[8,2048]{1,0:T(8,128)}, bf16[2,128,768]{2,1,0:T(8,128)(2,1)}, bf16[2,128,768]{2,1,0:T(8,128)(2,1)}, bf16[2,1...) custom-call(bf16[1024,2048]{1,0:T(8,128)(2,1)} %get-tuple-element.112.refs_0_, bf16[256,2048]{1,0:T(8,128)(2,1)} %refs_1_.3, ...), custom_call_target="tpu_custom_call" | custom-call | bytes 134217728 | tf_op jit(solution)/shard_map/exchange_last/pallas_call | solution.py:838
  642.3 1.0 copy-done.18
  643.3 1.0 copy-done.19
  644.3 0.9 copy-done.20
  645.2 0.8 copy-done.22
  646.1 17.1 %adam_matrices.1 = (f32[1,128]{1,0:T(1,128)S(1)}, bf16[256,2048]{1,0:T(8,128)(2,1)}, f32[256,2048]{1,0:T(8,128)}, f32[2,2048]{1,0:T(2,128)}, f32[2,2048]{1,0:T(2...) custom-call(bf16[2,128,768]{2,1,0:T(8,128)(2,1)S(1)} %copy-done.14, ...), custom_call_target="tpu_custom_call" | custom-call | flops 33554432 | bytes 41943040 | tf_op jit(solution)/shard_map/adam_matrices/pallas_call | solution.py:1268
  663.1 0.5 slice_bitcast_fusion
  (61 shorter events, 0.2 us)
Async XLA Ops:
  7.2 269.4 %all-gather.2.cloned.1.call-start = ((), (), s32[]{:S(2)}) async-start(), calls=%async_computation | async-start | bytes 33423360 | tf_op jit(solution)/shard_map/all_gather | solution.py:1412
  8.7 11.0 %copy-start.21 = (f32[1,2048]{1,0:T(1,128)}, f32[1,2048]{1,0:T(1,128)S(1)}, u32[]{:S(2)}) copy-start(f32[1,2048]{1,0:T(1,128)S(1)} %get-tuple-element.156.refs_7_.refs_2_) | copy-start | bytes 24580
  8.7 1.2 copy-start
  9.9 1.0 copy-start.1
  10.9 1.0 copy-start.3
  12.0 1.0 copy-start.5
  13.7 8.6 %copy-start.34 = (s32[16]{0:T(128)S(1)}, s32[16]{0:T(128)}, u32[]{:S(2)}) copy-start(s32[16]{0:T(128)} %refs_0_.3) | copy-start | bytes 196
  13.7 9.4 %copy-start.35 = (s32[16]{0:T(128)S(1)}, s32[16]{0:T(128)}, u32[]{:S(2)}) copy-start(s32[16]{0:T(128)} %param.31) | copy-start | bytes 196
  19.7 1.0 copy-start.7
  22.3 143.9 %copy-start.30 = (f32[2,128]{1,0:T(2,128)S(1)}, f32[2,128]{1,0:T(2,128)}, u32[]{:S(2)}) copy-start(f32[2,128]{1,0:T(2,128)} %refs_15_.1) | copy-start | bytes 3076
  188.5 1.0 copy-start.6
  497.3 144.9 %copy-start.2 = (f32[128,1024]{1,0:T(8,128)S(1)}, f32[128,1024]{1,0:T(8,128)}, u32[]{:S(2)}) copy-start(f32[128,1024]{1,0:T(8,128)} %refs_27_.1) | copy-start | bytes 1572868
  497.3 144.9 %copy-start.4 = (f32[2,128,512]{2,1,0:T(8,128)S(1)}, f32[2,128,512]{2,1,0:T(8,128)}, u32[]{:S(2)}) copy-start(f32[2,128,512]{2,1,0:T(8,128)} %refs_30_.1) | copy-start | bytes 1572868
  497.3 144.9 %copy-start.9 = (f32[128,1024]{1,0:T(8,128)S(1)}, f32[128,1024]{1,0:T(8,128)}, u32[]{:S(2)}) copy-start(f32[128,1024]{1,0:T(8,128)} %refs_28_.1) | copy-start | bytes 1572868
  497.3 144.9 %copy-start.10 = (f32[128,1024]{1,0:T(8,128)S(1)}, f32[128,1024]{1,0:T(8,128)}, u32[]{:S(2)}) copy-start(f32[128,1024]{1,0:T(8,128)} %refs_29_.1) | copy-start | bytes 1572868
  497.3 144.9 %copy-start.11 = (f32[2,128,512]{2,1,0:T(8,128)S(1)}, f32[2,128,512]{2,1,0:T(8,128)}, u32[]{:S(2)}) copy-start(f32[2,128,512]{2,1,0:T(8,128)} %refs_31_.1) | copy-start | bytes 1572868
  497.3 144.9 %copy-start.12 = (f32[2,128,512]{2,1,0:T(8,128)S(1)}, f32[2,128,512]{2,1,0:T(8,128)}, u32[]{:S(2)}) copy-start(f32[2,128,512]{2,1,0:T(8,128)} %refs_32_.1) | copy-start | bytes 1572868
  497.3 144.9 %copy-start.14 = (bf16[2,128,768]{2,1,0:T(8,128)(2,1)S(1)}, bf16[2,128,768]{2,1,0:T(8,128)(2,1)}, u32[]{:S(2)}) copy-start(bf16[2,128,768]{2,1,0:T(8,128)(2,1)} %get-tuple-element.106.refs_0_) | copy-start | bytes 1179652
  497.3 144.9 %copy-start.15 = (bf16[2,128,768]{2,1,0:T(8,128)(2,1)S(1)}, bf16[2,128,768]{2,1,0:T(8,128)(2,1)}, u32[]{:S(2)}) copy-start(bf16[2,128,768]{2,1,0:T(8,128)(2,1)} %get-tuple-element.107.refs_1_) | copy-start | bytes 1179652
  497.3 144.9 %copy-start.16 = (bf16[2,128,768]{2,1,0:T(8,128)(2,1)S(1)}, bf16[2,128,768]{2,1,0:T(8,128)(2,1)}, u32[]{:S(2)}) copy-start(bf16[2,128,768]{2,1,0:T(8,128)(2,1)} %get-tuple-element.108.refs_2_) | copy-start | bytes 1179652
  497.3 144.9 %copy-start.17 = (bf16[2,128,768]{2,1,0:T(8,128)(2,1)S(1)}, bf16[2,128,768]{2,1,0:T(8,128)(2,1)}, u32[]{:S(2)}) copy-start(bf16[2,128,768]{2,1,0:T(8,128)(2,1)} %get-tuple-element.109.refs_3_) | copy-start | bytes 1179652
  497.3 144.9 %copy-start.23 = (f32[2,2048]{1,0:T(2,128)S(1)}, f32[2,2048]{1,0:T(2,128)}, u32[]{:S(2)}) copy-start(f32[2,2048]{1,0:T(2,128)} %refs_12_.1) | copy-start | bytes 49156
  497.3 144.9 %copy-start.24 = (f32[2,2048]{1,0:T(2,128)S(1)}, f32[2,2048]{1,0:T(2,128)}, u32[]{:S(2)}) copy-start(f32[2,2048]{1,0:T(2,128)} %refs_13_.1) | copy-start | bytes 49156
  497.4 144.9 %copy-start.25 = (f32[2,2048]{1,0:T(2,128)S(1)}, f32[2,2048]{1,0:T(2,128)}, u32[]{:S(2)}) copy-start(f32[2,2048]{1,0:T(2,128)} %refs_14_.1) | copy-start | bytes 49156
  497.4 144.9 %copy-start.27 = (f32[128,8]{0,1:T(8,128)S(1)}, f32[128,8]{0,1:T(8,128)}, u32[]{:S(2)}) copy-start(f32[128,8]{0,1:T(8,128)} %param.44) | copy-start | bytes 12292
  497.4 144.9 %copy-start.28 = (f32[128,8]{0,1:T(8,128)S(1)}, f32[128,8]{0,1:T(8,128)}, u32[]{:S(2)}) copy-start(f32[128,8]{0,1:T(8,128)} %param.45) | copy-start | bytes 12292
  497.4 144.9 %copy-start.29 = (f32[128,8]{0,1:T(8,128)S(1)}, f32[128,8]{0,1:T(8,128)}, u32[]{:S(2)}) copy-start(f32[128,8]{0,1:T(8,128)} %param.46) | copy-start | bytes 12292
  497.4 144.9 %copy-start.31 = (f32[2,128]{1,0:T(2,128)S(1)}, f32[2,128]{1,0:T(2,128)}, u32[]{:S(2)}) copy-start(f32[2,128]{1,0:T(2,128)} %refs_16_.1) | copy-start | bytes 3076
  497.4 144.9 %copy-start.32 = (f32[2,128]{1,0:T(2,128)S(1)}, f32[2,128]{1,0:T(2,128)}, u32[]{:S(2)}) copy-start(f32[2,128]{1,0:T(2,128)} %refs_17_.1) | copy-start | bytes 3076
  642.3 1.0 copy-start.18
  643.3 1.0 copy-start.19
  644.3 0.9 copy-start.20
  (5 other events, 3.7 us)
Sparse Core Ops, SparseCore 0:
  22.5 254.0 all-gather.1
where the time goes:
time: 680 us; the launch traced here: 671 us
  Pallas kernels  628 us (92%)
  between operations  15.4 us (2%)
  local copies, waits for them, and re-layouts  15.1 us (2%)
  waiting for transfers between devices  10.1 us (1%)
    pallas_call x1, Pallas kernels, exchange_last(): pl.pallas_call(body, out_shape=[jax.ShapeDtypeStruct((size, MODEL_WIDTH),...  145 us
    pallas_call x1, Pallas kernels, gather_attention(): pl.pallas_call(gather_kernel, out_shape=[jax.ShapeDtypeStruct((MODEL_WIDT...  141 us
    pallas_call x1, Pallas kernels, exchange_backward(): pl.pallas_call(body, out_shape=[jax.ShapeDtypeStruct((size, MODEL_WIDTH),...  135 us
    pallas_call x1, Pallas kernels, exchange_forward(): pl.pallas_call(forward_kernel, out_shape=[jax.ShapeDtypeStruct((size, MOD...  77 us
    pallas_call x2, Pallas kernels, attention_call(): pl.pallas_call(body, grid=(sequences,), out_shape=outputs, in_specs=[SCAL...  57.4 us
    pallas_call x1, Pallas kernels, feedforward(): pl.pallas_call(body, grid_spec=pltpu.PrefetchScalarGridSpec(num_scalar_pr...  49.5 us
    pallas_call x1, Pallas kernels, adam_matrices(): pl.pallas_call(body, out_shape=like([inverse, *extra, *states]), in_specs...  17.1 us
  transfers between devices with their start and end apart: 1, of which 1 were waited for; matrix products, arithmetic and copies ran while one was open for 0% of the time, Pallas kernels for 36%

commit v1 on v0

--- a/solution.py
+++ b/solution.py
@@ -434,7 +434,7 @@
 
 def settings(collective):
     return pltpu.CompilerParams(
-        collective_id=collective, has_side_effects=True, vmem_limit_bytes=56 * 2**20
+        collective_id=collective, has_side_effects=True, vmem_limit_bytes=60 * 2**20
     )
 
 
@@ -926,7 +926,7 @@
         ),
         out_shape=[jax.ShapeDtypeStruct((count, hidden), low)] * 3
         + [jax.ShapeDtypeStruct((count, MODEL_WIDTH), low)] * 2,
-        compiler_params=pltpu.CompilerParams(vmem_limit_bytes=52 * 2**20),
+        compiler_params=pltpu.CompilerParams(vmem_limit_bytes=60 * 2**20),
         cost_estimate=pl.CostEstimate(
             flops=12 * count * MODEL_WIDTH * hidden,
             bytes_accessed=48 * 2**20,
@@ -957,14 +957,20 @@
     return jax.nn.sigmoid(logit)
 
 
-def probabilities(queries, keys, start, valid_count, piece_start):
-    raw = dot(queries, keys, 1, 1) * HEAD_WIDTH ** (-0.5)
-    row = start + lax.broadcasted_iota(jnp.int32, raw.shape, 0)
-    column = lax.broadcasted_iota(jnp.int32, raw.shape, 1)
-    last = piece_start + PIC
-    inside = (row >= piece_start) & (row < last) & (column >= piece_start) & (column < last)
-    allowed = (column < valid_count) & ((column <= row) | inside)
-    scores = jnp.where(allowed, raw, masked_score)
+def mask_rows(mask, valid_count, piece_start):
+    length = mask.shape[0]
+    for start in range(0, length, QUERY_ROWS):
+        shape = (QUERY_ROWS, length)
+        row = start + lax.broadcasted_iota(jnp.int32, shape, 0)
+        column = lax.broadcasted_iota(jnp.int32, shape, 1)
+        last = piece_start + PIC
+        inside = (row >= piece_start) & (row < last) & (column >= piece_start) & (column < last)
+        allowed = (column < valid_count) & ((column <= row) | inside)
+        mask[start : start + QUERY_ROWS, :] = jnp.where(allowed, 0.0, masked_score)
+
+
+def probabilities(queries, keys, mask):
+    scores = dot(queries, keys, 1, 1) * HEAD_WIDTH ** (-0.5) + mask
     expos = jnp.exp(scores - jnp.max(scores, axis=-1, keepdims=True))
     return expos * (1.0 / jnp.sum(expos, axis=-1, keepdims=True))
 
@@ -973,9 +979,10 @@
 
 
 def attention_forward_kernel(
-    groups, share, valid, start, rows_in, weights, gains, cosine, sine, pre, gated, partial
+    groups, share, valid, start, rows_in, weights, gains, cosine, sine, pre, gated, partial, mask
 ):
     sequence = pl.program_id(0)
+    mask_rows(mask, valid[sequence], start[sequence])
     heads = groups * share
     length, projected = pre.shape
     for column in range(0, projected, 3 * HEAD_WIDTH):
@@ -990,7 +997,7 @@
                 queries = head_rows(
                     pre[rows, head_at(head)], gains[0:1, :], cosine[rows, :], sine[rows, :]
                 )
-                probs = probabilities(queries, keys, at, valid[sequence], start[sequence])
+                probs = probabilities(queries, keys, mask[rows, :])
                 mixed = dot(probs.astype(low), values, 1, 0)
                 gate = gate_column(pre[rows, head_at(heads + 2 * groups)], head)
                 gated[rows, head_at(head)] = (mixed * gate).astype(low)
@@ -1002,9 +1009,10 @@
 
 def attention_backward_kernel(
     groups, share, valid, start, pre, rows_in, weights, gains, cosine, sine,
-    grads, gain_grads, partial, upstream,
+    grads, gain_grads, partial, upstream, mask,
 ):
     sequence = pl.program_id(0)
+    mask_rows(mask, valid[sequence], start[sequence])
     heads = groups * share
     length, projected = pre.shape
     upstream[...] = dot(rows_in[...], weights[:, projected:], 1, 0)
@@ -1026,7 +1034,7 @@
                 rows = slice(at, at + QUERY_ROWS)
                 query_pre = pre[rows, head_at(head)]
                 queries = head_rows(query_pre, gains[0:1, :], cosine[rows, :], sine[rows, :])
-                probs = probabilities(queries, keys, at, valid[sequence], start[sequence])
+                probs = probabilities(queries, keys, mask[rows, :])
                 probs_low = probs.astype(low)
                 mixed = dot(probs_low, values, 1, 0)
                 gate = gate_column(pre[rows, head_at(heads + 2 * groups)], head)
@@ -1084,7 +1092,7 @@
         in_specs=[SCALARS, SCALARS, *specs],
         out_specs=out_specs,
         scratch_shapes=scratch,
-        compiler_params=pltpu.CompilerParams(vmem_limit_bytes=52 * 2**20),
+        compiler_params=pltpu.CompilerParams(vmem_limit_bytes=60 * 2**20),
         cost_estimate=pl.CostEstimate(
             flops=2**33, bytes_accessed=24 * 2**20, transcendentals=2**21
         ),
@@ -1119,7 +1127,7 @@
             jax.ShapeDtypeStruct((count, MODEL_WIDTH), low),
         ],
         [sequence_block(size, length) for size in (projected, columns, MODEL_WIDTH)],
-        [],
+        [pltpu.VMEM((length, length), wide)],
         (valid, start, rows, weights, gains, cosine, sine),
     )
 
@@ -1150,7 +1158,7 @@
             fixed_block(2, HEAD_WIDTH),
             sequence_block(MODEL_WIDTH, length),
         ],
-        [pltpu.VMEM((length, columns), wide)],
+        [pltpu.VMEM((length, columns), wide), pltpu.VMEM((length, length), wide)],
         (valid, start, pre, rows, weights, gains, cosine, sine),
     )
 
@@ -1277,7 +1285,7 @@
             pltpu.SemaphoreType.DMA((2, len(states))),
             pltpu.SemaphoreType.DMA((2, len(sums) + len(extra))),
         ],
-        compiler_params=pltpu.CompilerParams(vmem_limit_bytes=48 * 2**20),
+        compiler_params=pltpu.CompilerParams(vmem_limit_bytes=60 * 2**20),
         cost_estimate=pl.CostEstimate(
             flops=2**25, bytes_accessed=40 * 2**20, transcendentals=2**21
         ),
@@ -1285,10 +1293,16 @@
     )(*sums.values(), stats, inverse, *extra, *states)
 
 
-def prepare_kernel(
-    sizes, query, keyvalue, headgate, output, gateup, down, tokens, gain,
-    attention, normed, large, small,
-):
+def prepare_kernel(sizes, *refs):
+    given, (attention, normed, large, small), refs = refs[:8], refs[8:12], refs[12:]
+    loads = [
+        pltpu.make_async_copy(value, refs[i], refs[8].at[i]) for i, value in enumerate(given)
+    ]
+    for load in loads:
+        load.start()
+    for load in loads:
+        load.wait()
+    query, keyvalue, headgate, output, gateup, down, tokens, gain = refs[:8]
     core = lax.axis_index("c")
     head_cols, group_cols = query.shape[1] // 2, keyvalue.shape[2] // 2
     edges = [head_cols, head_cols + group_cols, head_cols + 2 * group_cols]
@@ -1330,6 +1344,7 @@
 def prepare(sizes, query, keyvalue, headgate, output, gateup, down, tokens, gain):
     rows = query.shape[0]
     columns = query.shape[1] // 2 * 2 + keyvalue.shape[2] + HEAD_WIDTH
+    operands = (query, keyvalue, headgate, output, gateup, down, tokens, gain)
 
     def body(*refs):
         prepare_kernel(sizes, *refs)
@@ -1342,14 +1357,16 @@
             jax.ShapeDtypeStruct((2, rows, 3 * sizes[0]), low),
             jax.ShapeDtypeStruct((2, rows, 3 * sizes[1]), low),
         ],
-        in_specs=[VMEM] * 8,
+        in_specs=[ANY] * 8,
         out_specs=[VMEM] * 4,
-        compiler_params=pltpu.CompilerParams(vmem_limit_bytes=48 * 2**20),
+        scratch_shapes=[pltpu.VMEM(value.shape, value.dtype) for value in operands]
+        + [pltpu.SemaphoreType.DMA((8,))],
+        compiler_params=pltpu.CompilerParams(vmem_limit_bytes=60 * 2**20),
         cost_estimate=pl.CostEstimate(
             flops=2**22, bytes_accessed=12 * 2**20, transcendentals=0
         ),
         name="prepare",
-    )(query, keyvalue, headgate, output, gateup, down, tokens, gain)
+    )(*operands)
 
 
 def local(

time: 680 us -> 673 us (0.990)
  local copies, waits for them, and re-layouts: 15.1 us -> 4.24 us
    unnamed x72 -> x4, local copies, waits for them, and re-layouts: 13.1 us -> 0.01 us
  transfers between devices with their start and end apart: 1 -> 1, of which waited for: 1 -> 1; matrix products, arithmetic and copies ran while one was open for 0% -> 1% of each run, Pallas kernels for 36% -> 36%
where the time goes in v1:
time: 673 us; the launch traced here: 664 us
  Pallas kernels  632 us (94%)
  between operations  15.1 us (2%)
  waiting for transfers between devices  9.48 us (1%)
    pallas_call x1, Pallas kernels, exchange_last(): pl.pallas_call(body, out_shape=[jax.ShapeDtypeStruct((size, MODEL_WIDTH),...  145 us
    pallas_call x1, Pallas kernels, gather_attention(): pl.pallas_call(gather_kernel, out_shape=[jax.ShapeDtypeStruct((MODEL_WIDT...  141 us
    pallas_call x1, Pallas kernels, exchange_backward(): pl.pallas_call(body, out_shape=[jax.ShapeDtypeStruct((size, MODEL_WIDTH),...  135 us
    pallas_call x1, Pallas kernels, exchange_forward(): pl.pallas_call(forward_kernel, out_shape=[jax.ShapeDtypeStruct((size, MOD...  77.2 us
    pallas_call x2, Pallas kernels, attention_call(): pl.pallas_call(body, grid=(sequences,), out_shape=outputs, in_specs=[SCAL...  57.4 us
    pallas_call x1, Pallas kernels, feedforward(): pl.pallas_call(body, grid_spec=pltpu.PrefetchScalarGridSpec(num_scalar_pr...  49.7 us
    pallas_call x1, Pallas kernels, adam_matrices(): pl.pallas_call(body, out_shape=like([inverse, *extra, *states]), in_specs...  19.3 us
  transfers between devices with their start and end apart: 1, of which 1 were waited for; matrix products, arithmetic and copies ran while one was open for 1% of the time, Pallas kernels for 36%

profile of v1, /device:TPU:0, one launch (start us, length us, event | category | flops | bytes accessed | tf_op | source)
XLA Modules:
  0.0 663.5 jit_solution(15358494790669845271)
XLA Ops:
  7.2 0.0 all-gather.2.cloned.1.call-start
  7.2 1.4 fusion.3
  8.7 0.0 copy-start
  8.7 0.0 copy-start.1
  8.7 7.6 %prepare.1 = (bf16[2,128,1664]{2,1,0:T(8,128)(2,1)}, bf16[256,2048]{1,0:T(8,128)(2,1)}, bf16[2,128,3840]{2,1,0:T(8,128)(2,1)}, bf16[2,128,768]{2,1,0:T(8,128)(2,1)}) custom-call(f32[128,1024]{1,0:T(8,128)} %refs_27_.1, f32[2,128,512]{2,1,0:T(8,128)} %refs_30_.1, f32[8,128]{1,0:T(8,128)} %bitcast.9, f32[1024,128]{1,0:T(8,128)} %refs_33_.1, ...), custom_call_target="tpu_custom_call" | custom-call | flops 4194304 | bytes 12582912 | tf_op jit(solution)/shard_map/prepare/pallas_call | solution.py:1352
  16.2 0.0 all-gather.2.cloned.1.call-update
  16.3 0.0 copy-done
  16.3 0.6 reduce_sum.9
  16.9 0.6 dynamic_slice.6.refs_0_
  17.5 0.0 copy-done.1
  17.5 0.6 dynamic_slice.7.refs_1_
  18.8 140.9 %gather_attention.1 = (bf16[2048,1664]{1,0:T(8,128)(2,1)}, bf16[1024,2048]{1,0:T(8,128)(2,1)}, bf16[1024,2048]{1,0:T(8,128)(2,1)}) custom-call(bf16[2,128,1664]{2,1,0:T(8,128)(2,1)} %get-tuple-element.91.pieces, bf16[256,2048]{1,0:T(8,128)(2,1)} %get-tuple-element.92.first, bf16[256,2048]{1,0:T(8,128)(2,1)} %refs_4_.5), custom_call_target="tpu_custom_call" | custom-call | bytes 67108864 | tf_op jit(solution)/shard_map/gather_attention/pallas_call | solution.py:540
  159.7 1.0 fusion.2
  160.7 1.0 pad_maximum_fusion
  161.7 22.3 %attention_forward.1 = (f32[1024,1152]{1,0:T(8,128)}, bf16[1024,512]{1,0:T(8,128)(2,1)}, bf16[1024,2048]{1,0:T(8,128)(2,1)}) custom-call(s32[2]{0:T(128)} %dynamic_slice.6.refs_0_, s32[2]{0:T(128)} %dynamic_slice.7.refs_1_, bf16[1024,2048]{1,0:T(8,128)(2,1)} %get-tuple-element.93.refs_2_.refs_10_, bf16[2048,1664]{1,0:T(8,128)(2,1)} %get-tuple-element.94.refs_3_.refs_4_, ...), custom_call_target="tpu_custom_call" | custom-call | flops 8589934592 | bytes 25165824 | tf_op jit(solution)/shard_map/attention_forward/pallas_call | solution.py:1088
  184.1 77.2 %exchange_forward.1 = (f32[256,2048]{1,0:T(8,128)}, f32[2,2048]{1,0:T(2,128)}, bf16[1024,2048]{1,0:T(8,128)(2,1)}, bf16[2048,768]{1,0:T(8,128)(2,1)}) custom-call(s32[16]{0:T(128)} %refs_0_.3, bf16[1024,2048]{1,0:T(8,128)(2,1)} %get-tuple-element.95.partial, bf16[256,2048]{1,0:T(8,128)(2,1)} %refs_1_.3, f32[1,2048]{1,0:T(1,128)} %get-tuple-element.155.gain.refs_5_, ...), custom_call_target="tpu_custom_call" | custom-call | bytes 67108864 | tf_op jit(solution)/shard_map/exchange_forward/pallas_call | solution.py:610
  261.2 9.5 %all-gather.2.cloned.1.call-done.refs_3_ = bf16[2,2048,3840]{2,1,0:T(8,128)(2,1)} async-done(((bf16[2,128,3840]{2,1,0:T(8,128)(2,1)}), bf16[2,2048,3840]{2,1,0:T(8,128)(2,1)}) %all-gather.2.cloned.1.call-update) | async-done | bytes 31457296 | tf_op jit(solution)/shard_map/all_gather | solution.py:1429
  270.7 49.7 %feedforward.1 = (bf16[1024,1536]{1,0:T(8,128)(2,1)}, bf16[1024,1536]{1,0:T(8,128)(2,1)}, bf16[1024,1536]{1,0:T(8,128)(2,1)}, bf16[1024,2048]{1,0:T(8,128)(2,1)}, bf16[1024,2048]{1,0:T(8,128)(2,1)}) custom-call(s32[1]{0:T(128)} %bitcast.refs_0_, bf16[1024,2048]{1,0:T(8,128)(2,1)} %get-tuple-element.97.refs_1_.refs_6_, ...), custom_call_target="tpu_custom_call" | custom-call | flops 38654705664 | bytes 50331648 | tf_op jit(solution)/shard_map/feedforward/pallas_call | solution.py:910
  320.4 135.4 %exchange_backward.1 = (f32[256,2048]{1,0:T(8,128)}, f32[1,2048]{1,0:T(1,128)}, bf16[256,2048]{1,0:T(8,128)(2,1)}, f32[1,2048]{1,0:T(1,128)}, bf16[1024,2048]{1,...) custom-call(s32[16]{0:T(128)} %refs_0_.3, ...), custom_call_target="tpu_custom_call" | custom-call | bytes 134217728 | tf_op jit(solution)/shard_map/exchange_backward/pallas_call | solution.py:719
  455.8 35.1 %attention_backward.1 = (bf16[1024,1152]{1,0:T(8,128)(2,1)}, f32[2,128]{1,0:T(2,128)}, bf16[1024,2048]{1,0:T(8,128)(2,1)}) custom-call(s32[2]{0:T(128)} %dynamic_slice.6.refs_0_, s32[2]{0:T(128)} %dynamic_slice.7.refs_1_, f32[1024,1152]{1,0:T(8,128)} %get-tuple-element.110.refs_2_, bf16[1024,2048]{1,0:T(8,128)(2,1)} %get-tuple-element.111.refs_3_.refs_12_, ...), custom_call_target="tpu_custom_call" | custom-call | flops 8589934592 | bytes 25165824 | tf_op jit(solution)/shard_map/attention_backward/pallas_call | solution.py:1088
  490.9 144.5 %exchange_last.1 = (f32[256,2048]{1,0:T(8,128)}, f32[8,2048]{1,0:T(8,128)}, bf16[2,128,768]{2,1,0:T(8,128)(2,1)}, bf16[2,128,768]{2,1,0:T(8,128)(2,1)}, bf16[2,1...) custom-call(bf16[1024,2048]{1,0:T(8,128)(2,1)} %get-tuple-element.112.refs_0_, bf16[256,2048]{1,0:T(8,128)(2,1)} %refs_1_.3, ...), custom_call_target="tpu_custom_call" | custom-call | bytes 134217728 | tf_op jit(solution)/shard_map/exchange_last/pallas_call | solution.py:838
  635.4 0.5 broadcast_in_dim.9.refs_9_
  636.0 19.3 %adam_matrices.1 = (f32[1,128]{1,0:T(1,128)}, bf16[256,2048]{1,0:T(8,128)(2,1)}, f32[256,2048]{1,0:T(8,128)}, f32[2,2048]{1,0:T(2,128)}, f32[2,2048]{1,0:T(2,128...) custom-call(bf16[2,128,768]{2,1,0:T(8,128)(2,1)} %get-tuple-element., ...), custom_call_target="tpu_custom_call" | custom-call | flops 33554432 | bytes 41943040 | tf_op jit(solution)/shard_map/adam_matrices/pallas_call | solution.py:1276
  655.3 1.1 slice_bitcast_fusion
  (1 shorter events, 0.0 us)
Async XLA Ops:
  7.2 263.5 %all-gather.2.cloned.1.call-start = ((), (), s32[]{:S(2)}) async-start(), calls=%async_computation | async-start | bytes 33423360 | tf_op jit(solution)/shard_map/all_gather | solution.py:1429
  8.7 7.6 %copy-start = (s32[16]{0:T(128)S(1)}, s32[16]{0:T(128)}, u32[]{:S(2)}) copy-start(s32[16]{0:T(128)} %refs_0_.3) | copy-start | bytes 196
  8.7 8.8 %copy-start.1 = (s32[16]{0:T(128)S(1)}, s32[16]{0:T(128)}, u32[]{:S(2)}) copy-start(s32[16]{0:T(128)} %param.31) | copy-start | bytes 196
Sparse Core Ops, SparseCore 0:
  16.4 254.2 all-gather.1

commit v2 on v1

--- a/solution.py
+++ b/solution.py
@@ -1450,8 +1450,7 @@
     gate_grad, up_grad, hidden_low, second_partial, feedforward_partial = feedforward(
         core[None], second_full, output_grad_full, large_both, small_full
     )
-    half = hidden_here // 2
-    pieces = [(0, half), (half, hidden_here - half)]
+    pieces = [(0, hidden_here)]
     middle_grad, second_gain_grad, block_output, output_squares, attention_grad, *sums = (
         exchange_backward(
             valid_len,
@@ -1492,7 +1491,7 @@
     input_rate = MODEL_WIDTH ** (-0.5)
     down_rate = FF ** (-0.5)
     output_rate = max(QUERY_HEADS * HEAD_WIDTH // 128, 4) ** (-0.5)
-    widths = [half, hidden_here - half]
+    widths = [hidden_here]
 
     def parts_of(name):
         return [(f"{name} {index}", 0, width) for index, width in enumerate(widths)]
@@ -1512,7 +1511,7 @@
         ),
         (True, output_rate, [[("output", 0, head_cols)]]),
     ]
-    names = ["gate 0", "gate 1", "up 0", "up 1", "down 0", "down 1", "projected", "output"]
+    names = ["gate 0", "up 0", "down 0", "projected", "output"]
     sums = dict(zip(names, [*sums, *more]))
     scales, block_output, tokens_grad, *updated = adam_matrices(
         layouts,

time: 673 us -> 671 us (level)
  no operation moved by 1% of the time
where the time goes in v2:
time: 671 us; the launch traced here: 662 us
  Pallas kernels  630 us (94%)
  between operations  15.3 us (2%)
  waiting for transfers between devices  9.48 us (1%)
    pallas_call x1, Pallas kernels, exchange_last(): pl.pallas_call(body, out_shape=[jax.ShapeDtypeStruct((size, MODEL_WIDTH),...  144 us
    pallas_call x1, Pallas kernels, gather_attention(): pl.pallas_call(gather_kernel, out_shape=[jax.ShapeDtypeStruct((MODEL_WIDT...  141 us
    pallas_call x1, Pallas kernels, exchange_backward(): pl.pallas_call(body, out_shape=[jax.ShapeDtypeStruct((size, MODEL_WIDTH),...  134 us
    pallas_call x1, Pallas kernels, exchange_forward(): pl.pallas_call(forward_kernel, out_shape=[jax.ShapeDtypeStruct((size, MOD...  77.2 us
    pallas_call x2, Pallas kernels, attention_call(): pl.pallas_call(body, grid=(sequences,), out_shape=outputs, in_specs=[SCAL...  57.2 us
    pallas_call x1, Pallas kernels, feedforward(): pl.pallas_call(body, grid_spec=pltpu.PrefetchScalarGridSpec(num_scalar_pr...  49.7 us
    pallas_call x1, Pallas kernels, adam_matrices(): pl.pallas_call(body, out_shape=like([inverse, *extra, *states]), in_specs...  19.2 us
  transfers between devices with their start and end apart: 1, of which 1 were waited for; matrix products, arithmetic and copies ran while one was open for 1% of the time, Pallas kernels for 36%

profile of v2, /device:TPU:0, one launch (start us, length us, event | category | flops | bytes accessed | tf_op | source)
XLA Modules:
  0.0 661.9 jit_solution(16306045926816391726)
XLA Ops:
  7.2 0.0 all-gather.2.cloned.1.call-start
  7.2 1.4 fusion.3
  8.7 0.0 copy-start
  8.7 0.0 copy-start.1
  8.7 7.6 %prepare.1 = (bf16[2,128,1664]{2,1,0:T(8,128)(2,1)}, bf16[256,2048]{1,0:T(8,128)(2,1)}, bf16[2,128,3840]{2,1,0:T(8,128)(2,1)}, bf16[2,128,768]{2,1,0:T(8,128)(2,1)}) custom-call(f32[128,1024]{1,0:T(8,128)} %refs_24_.1, f32[2,128,512]{2,1,0:T(8,128)} %refs_27_.1, f32[8,128]{1,0:T(8,128)} %bitcast.9, f32[1024,128]{1,0:T(8,128)} %refs_30_.1, ...), custom_call_target="tpu_custom_call" | custom-call | flops 4194304 | bytes 12582912 | tf_op jit(solution)/shard_map/prepare/pallas_call | solution.py:1352
  16.2 0.0 all-gather.2.cloned.1.call-update
  16.3 0.0 copy-done
  16.3 0.6 reduce_sum.9
  16.9 0.6 dynamic_slice.6.refs_0_
  17.5 0.0 copy-done.1
  17.5 0.6 dynamic_slice.7.refs_1_
  18.8 140.9 %gather_attention.1 = (bf16[2048,1664]{1,0:T(8,128)(2,1)}, bf16[1024,2048]{1,0:T(8,128)(2,1)}, bf16[1024,2048]{1,0:T(8,128)(2,1)}) custom-call(bf16[2,128,1664]{2,1,0:T(8,128)(2,1)} %get-tuple-element.88.pieces, bf16[256,2048]{1,0:T(8,128)(2,1)} %get-tuple-element.89.first, bf16[256,2048]{1,0:T(8,128)(2,1)} %refs_4_.5), custom_call_target="tpu_custom_call" | custom-call | bytes 67108864 | tf_op jit(solution)/shard_map/gather_attention/pallas_call | solution.py:540
  159.7 1.0 fusion.2
  160.7 1.0 pad_maximum_fusion
  161.7 22.3 %attention_forward.1 = (f32[1024,1152]{1,0:T(8,128)}, bf16[1024,512]{1,0:T(8,128)(2,1)}, bf16[1024,2048]{1,0:T(8,128)(2,1)}) custom-call(s32[2]{0:T(128)} %dynamic_slice.6.refs_0_, s32[2]{0:T(128)} %dynamic_slice.7.refs_1_, bf16[1024,2048]{1,0:T(8,128)(2,1)} %get-tuple-element.90.refs_2_.refs_10_, bf16[2048,1664]{1,0:T(8,128)(2,1)} %get-tuple-element.91.refs_3_.refs_4_, ...), custom_call_target="tpu_custom_call" | custom-call | flops 8589934592 | bytes 25165824 | tf_op jit(solution)/shard_map/attention_forward/pallas_call | solution.py:1088
  184.1 77.2 %exchange_forward.1 = (f32[256,2048]{1,0:T(8,128)}, f32[2,2048]{1,0:T(2,128)}, bf16[1024,2048]{1,0:T(8,128)(2,1)}, bf16[2048,768]{1,0:T(8,128)(2,1)}) custom-call(s32[16]{0:T(128)} %refs_0_.3, bf16[1024,2048]{1,0:T(8,128)(2,1)} %get-tuple-element.92.partial, bf16[256,2048]{1,0:T(8,128)(2,1)} %refs_1_.3, f32[1,2048]{1,0:T(1,128)} %get-tuple-element.149.gain.refs_5_, ...), custom_call_target="tpu_custom_call" | custom-call | bytes 67108864 | tf_op jit(solution)/shard_map/exchange_forward/pallas_call | solution.py:610
  261.2 9.5 %all-gather.2.cloned.1.call-done.refs_3_ = bf16[2,2048,3840]{2,1,0:T(8,128)(2,1)} async-done(((bf16[2,128,3840]{2,1,0:T(8,128)(2,1)}), bf16[2,2048,3840]{2,1,0:T(8,128)(2,1)}) %all-gather.2.cloned.1.call-update) | async-done | bytes 31457296 | tf_op jit(solution)/shard_map/all_gather | solution.py:1429
  270.7 49.7 %feedforward.1 = (bf16[1024,1536]{1,0:T(8,128)(2,1)}, bf16[1024,1536]{1,0:T(8,128)(2,1)}, bf16[1024,1536]{1,0:T(8,128)(2,1)}, bf16[1024,2048]{1,0:T(8,128)(2,1)}, bf16[1024,2048]{1,0:T(8,128)(2,1)}) custom-call(s32[1]{0:T(128)} %bitcast.refs_0_, bf16[1024,2048]{1,0:T(8,128)(2,1)} %get-tuple-element.94.refs_1_.refs_6_, ...), custom_call_target="tpu_custom_call" | custom-call | flops 38654705664 | bytes 50331648 | tf_op jit(solution)/shard_map/feedforward/pallas_call | solution.py:910
  320.4 134.3 %exchange_backward.1 = (f32[256,2048]{1,0:T(8,128)}, f32[1,2048]{1,0:T(1,128)}, bf16[256,2048]{1,0:T(8,128)(2,1)}, f32[1,2048]{1,0:T(1,128)}, bf16[1024,2048]{1,...) custom-call(s32[16]{0:T(128)} %refs_0_.3, bf16[1024,2048]{1,0:T(8,128)(2,1)} %get-tuple-element.98.refs_1_, ...), custom_call_target="tpu_custom_call" | custom-call | bytes 134217728 | tf_op jit(solution)/shard_map/exchange_backward/pallas_call | solution.py:719
  454.7 34.8 %attention_backward.1 = (bf16[1024,1152]{1,0:T(8,128)(2,1)}, f32[2,128]{1,0:T(2,128)}, bf16[1024,2048]{1,0:T(8,128)(2,1)}) custom-call(s32[2]{0:T(128)} %dynamic_slice.6.refs_0_, s32[2]{0:T(128)} %dynamic_slice.7.refs_1_, f32[1024,1152]{1,0:T(8,128)} %get-tuple-element.105.refs_2_, bf16[1024,2048]{1,0:T(8,128)(2,1)} %get-tuple-element.106.refs_3_.refs_12_, ...), custom_call_target="tpu_custom_call" | custom-call | flops 8589934592 | bytes 25165824 | tf_op jit(solution)/shard_map/attention_backward/pallas_call | solution.py:1088
  489.5 144.2 %exchange_last.1 = (f32[256,2048]{1,0:T(8,128)}, f32[8,2048]{1,0:T(8,128)}, bf16[2,128,1536]{2,1,0:T(8,128)(2,1)}, bf16[2,128,1152]{2,1,0:T(8,128)(2,1)}, bf16[2,128,512]{2,1,0:T(8,128)(2,1)}) custom-call(bf16[1024,2048]{1,0:T(8,128)(2,1)} %get-tuple-element.107.refs_0_, bf16[256,2048]{1,0:T(8,128)(2,1)} %refs_1_.3, ...), custom_call_target="tpu_custom_call" | custom-call | bytes 134217728 | tf_op jit(solution)/shard_map/exchange_last/pallas_call | solution.py:838
  633.7 0.5 broadcast_in_dim.9.refs_6_
  634.2 19.2 %adam_matrices.1 = (f32[1,128]{1,0:T(1,128)}, bf16[256,2048]{1,0:T(8,128)(2,1)}, f32[256,2048]{1,0:T(8,128)}, f32[2,2048]{1,0:T(2,128)}, f32[2,2048]{1,0:T(2,128...) custom-call(bf16[2,128,1536]{2,1,0:T(8,128)(2,1)} %get-tuple-element, ...), custom_call_target="tpu_custom_call" | custom-call | flops 33554432 | bytes 41943040 | tf_op jit(solution)/shard_map/adam_matrices/pallas_call | solution.py:1276
  653.5 1.1 slice_bitcast_fusion
  (1 shorter events, 0.0 us)
Async XLA Ops:
  7.2 263.5 %all-gather.2.cloned.1.call-start = ((), (), s32[]{:S(2)}) async-start(), calls=%async_computation | async-start | bytes 33423360 | tf_op jit(solution)/shard_map/all_gather | solution.py:1429
  8.7 7.6 %copy-start = (s32[16]{0:T(128)S(1)}, s32[16]{0:T(128)}, u32[]{:S(2)}) copy-start(s32[16]{0:T(128)} %refs_0_.3) | copy-start | bytes 196
  8.7 8.8 %copy-start.1 = (s32[16]{0:T(128)S(1)}, s32[16]{0:T(128)}, u32[]{:S(2)}) copy-start(s32[16]{0:T(128)} %param.31) | copy-start | bytes 196
Sparse Core Ops, SparseCore 0:
  16.4 254.2 all-gather.1
